TPU v7x, 128 devices: a whole 4x4x4 slice. The times are simulated.
128 devices in a mesh: seq: 16 (over x_hi, y, core), gate: 8 (over z, x_lo).
Axes of the slice: x: 4 (x_hi: 2, x_lo: 2; x = x_hi * 2 + x_lo), y: 4, z: 4, core: 2. Of those that a mesh axis runs over, the one named last changes fastest.
Arguments:
- tokens: bfloat16 [16384, 2048], P(('seq', 'gate')), may hold values from -6 to 6
- cotangent: bfloat16 [16384, 2048], P(('seq', 'gate')), may hold values from -6 to 6
- start_state: float32 [16, 4096], P('seq', 'gate'), may hold values from -6 to 6
- slot_table: int32 [16], P('gate'), may hold values from -1 to 9, as said below
- norm_gains: float32 [2, 2048], replicated, may hold values from 0.5 to 1.5
- gain_first: float32 [2, 2048], replicated, may hold values from -320 to 320
- gain_second: float32 [2, 2048], replicated, may hold values from 8.192 to 131.072
- block_params: float32 [10, 8, 256], replicated
- block_first: float32 [10, 8, 256], replicated, may hold values from -1024 to 1024
- block_second: float32 [10, 8, 256], replicated, may hold values from 245.76 to 1966.08
- input_weights: float32 [2, 2048, 4096], P(None, 'seq', 'gate'), may hold values from -0.125 to 0.125
- input_first: float32 [2, 2048, 4096], P(None, 'seq', 'gate'), may hold values from -112 to 112
- input_second: float32 [2, 2048, 4096], P(None, 'seq', 'gate'), may hold values from 0.73728 to 11.79648
- output_weights: float32 [4096, 2048], P('gate', 'seq'), may hold values from -0.375 to 0.375
- output_first: float32 [4096, 2048], P('gate', 'seq'), may hold values from -112 to 112
- output_second: float32 [4096, 2048], P('gate', 'seq'), may hold values from 0.73728 to 11.79648
- gate_weights: float32 [2, 16, 256, 256], P(None, 'gate', 'seq'), may hold values from -0.375 to 0.375
- gate_first: float32 [2, 16, 256, 256], P(None, 'gate', 'seq'), may hold values from -32 to 32
- gate_second: float32 [2, 16, 256, 256], P(None, 'gate', 'seq'), may hold values from 0.08192 to 1.31072
- hidden_weights: float32 [2, 2048, 6144], P(None, 'seq', 'gate'), may hold values from -0.125 to 0.125
- hidden_first: float32 [2, 2048, 6144], P(None, 'seq', 'gate'), may hold values from -112 to 112
- hidden_second: float32 [2, 2048, 6144], P(None, 'seq', 'gate'), may hold values from 0.73728 to 11.79648
- down_weights: float32 [6144, 2048], P('gate', 'seq'), may hold values from -0.15625 to 0.15625
- down_first: float32 [6144, 2048], P('gate', 'seq'), may hold values from -160 to 160
- down_second: float32 [6144, 2048], P('gate', 'seq'), may hold values from 2.048 to 32.768
Outputs:
- layer_output: bfloat16 [16384, 2048], P(('seq', 'gate'))
- tokens_gradient: float32 [16384, 2048], P(('seq', 'gate'))
- gain_moment: float32 [2, 2048], replicated
- gain_square: float32 [2, 2048], replicated
- gain_master: float32 [2, 2048], replicated
- block_moment: float32 [10, 8, 256], replicated
- block_square: float32 [10, 8, 256], replicated
- block_master: float32 [10, 8, 256], replicated
- input_moment: float32 [2, 2048, 4096], P(None, 'seq', 'gate')
- input_square: float32 [2, 2048, 4096], P(None, 'seq', 'gate')
- input_master: float32 [2, 2048, 4096], P(None, 'seq', 'gate')
- output_moment: float32 [4096, 2048], P('gate', 'seq')
- output_square: float32 [4096, 2048], P('gate', 'seq')
- output_master: float32 [4096, 2048], P('gate', 'seq')
- gate_moment: float32 [2, 16, 256, 256], P(None, 'gate', 'seq')
- gate_square: float32 [2, 16, 256, 256], P(None, 'gate', 'seq')
- gate_master: float32 [2, 16, 256, 256], P(None, 'gate', 'seq')
- hidden_moment: float32 [2, 2048, 6144], P(None, 'seq', 'gate')
- hidden_square: float32 [2, 2048, 6144], P(None, 'seq', 'gate')
- hidden_master: float32 [2, 2048, 6144], P(None, 'seq', 'gate')
- down_moment: float32 [6144, 2048], P('gate', 'seq')
- down_square: float32 [6144, 2048], P('gate', 'seq')
- down_master: float32 [6144, 2048], P('gate', 'seq')
Inputs may be any that keep to these rules, and one draw needn't show every extreme that they name: `slot_table`: each of the 10 block numbers stands in exactly one slot; slots 2 * g onward belong to index g of gate, which holds one or two live slots, the live ones first in its range.
All inputs are finite; a program needn't handle non-finite values.
Results may differ from a plain program's by a relative error of at most 0.028.
Values may be sent and summed in bfloat16 or wider, within the bound.
No kernel may reach another device: no remote copies, remote signals or barrier semaphores. Data moves between devices by JAX's collectives and lax.ppermute only.
A program may use at most 192 MiB of HBM per device.

v0:
```python
import jax
import jax.numpy as jnp
from jax import lax
from jax.sharding import PartitionSpec as P

NBLK = 10
BLOCK = 256
KERNEL = 4
STEP = 10


NORM_EPS = 1e-06
BETA_ONE = 0.9
BETA_TWO = 0.999
ADAM_EPS = 1e-08
MATRIX_RATE = 0.02
SMALL_RATE = 0.2
VECTOR_RATE = 0.8
MATRIX_DECAY = 0.1
HIGHEST = lax.Precision.HIGHEST


def in_order(parts, dim):
    shape = list(parts.shape[1:])
    shape[dim] *= parts.shape[0]
    return jnp.moveaxis(parts, 0, dim).reshape(shape)


def one_gather(arrays, axis, dims):
    line = jnp.concatenate([a.reshape(-1) for a in arrays])
    lines, at, outs = (lax.all_gather(line, axis), 0, [])
    for a, dim in zip(arrays, dims):
        parts = lines[:, at : at + a.size].reshape(-1, *a.shape)
        outs.append(in_order(parts, dim))
        at += a.size
    return tuple(outs)


def gather_turned(arrays, axis, dims):
    turned = [jnp.moveaxis(a, dim, 0) for a, dim in zip(arrays, dims)]
    widths = [t[0].size for t in turned]
    both = jnp.concatenate([t.reshape(-1, w) for t, w in zip(turned, widths)], axis=1)
    whole = lax.all_gather(both, axis, axis=0, tiled=True)
    parts = jnp.split(whole, [sum(widths[:k]) for k in range(1, len(widths))], axis=1)
    return tuple(
        (
            jnp.moveaxis(b.reshape(-1, *t.shape[1:]), 0, dim)
            for b, t, dim in zip(parts, turned, dims)
        )
    )


def in_blocks(shard, dim, length):
    before, after = (shard.shape[:dim], shard.shape[dim + 1 :])
    return jnp.moveaxis(shard.reshape(*before, length, -1, *after), dim, 0)


def sum_together(arrays, axis, dims):
    length = lax.axis_size(axis)
    parts = [in_blocks(a, dim, length) for a, dim in zip(arrays, dims)]
    lines = jnp.concatenate([b.reshape(length, -1) for b in parts], axis=1)
    rows = max(16, -(-lines.shape[1] // 1024) * 8)
    lines = jnp.pad(lines, ((0, 0), (0, rows * 128 - lines.shape[1]))).reshape(-1, 128)
    line, at, outs = (lax.psum_scatter(lines, axis, tiled=True).reshape(-1), 0, [])
    for b in parts:
        part = b[0]
        outs.append(line[at : at + part.size].reshape(part.shape))
        at += part.size
    return tuple(outs)


def scale_norm(values, gain):
    return values * lax.rsqrt(jnp.mean(values * values, axis=-1, keepdims=True) + NORM_EPS) * gain


def norm_back(values, gain, d_normed):
    inverse = lax.rsqrt(jnp.mean(values * values, axis=-1, keepdims=True) + NORM_EPS)
    scaled = gain * d_normed
    d_values = inverse * scaled - values * inverse**3 * jnp.mean(
        scaled * values, axis=-1, keepdims=True
    )
    d_gain = jnp.sum(d_normed * values * inverse, axis=0)
    return (d_values, d_gain)


def causal_taps(values, tap_weights, tap_bias):
    length = values.shape[0]
    padded = jnp.concatenate(
        [jnp.zeros((KERNEL - 1, values.shape[1]), jnp.float32), values], axis=0
    )
    running = jnp.zeros_like(values) + tap_bias
    for offset in range(KERNEL):
        running = (
            running
            + tap_weights[offset] * padded[KERNEL - 1 - offset : KERNEL - 1 - offset + length]
        )
    return running


def taps_back(values, d_filtered, tap_weights):
    length = values.shape[0]
    columns = values.shape[1]
    padded = jnp.concatenate([jnp.zeros((KERNEL - 1, columns), jnp.float32), values], axis=0)
    later = jnp.concatenate([d_filtered, jnp.zeros((KERNEL - 1, columns), jnp.float32)], axis=0)
    tap_grads = []
    d_values = jnp.zeros_like(values)
    for offset in range(KERNEL):
        tap_grads.append(
            jnp.sum(d_filtered * padded[KERNEL - 1 - offset : KERNEL - 1 - offset + length], axis=0)
        )
        d_values = d_values + tap_weights[offset] * later[offset : offset + length]
    return (d_values, jnp.stack(tap_grads), jnp.sum(d_filtered, axis=0))


def gating(gate_a, gate_i, filtered, decay_param):
    log_rate = -8.0 * jax.nn.sigmoid(gate_a) * jax.nn.softplus(-decay_param)
    decays = jnp.exp(log_rate)
    drives = jnp.sqrt(-jnp.expm1(2.0 * log_rate)) * jax.nn.sigmoid(gate_i) * filtered
    return (decays, drives)


def run_recurrence(decays, drives, initial):
    length = decays.shape[0]
    columns = decays.shape[1]
    block_rows = min(128, length)

    def compose(earlier, later):
        return (later[0] * earlier[0], later[0] * earlier[1] + later[1])

    def one_block(carry_state, block_pair):
        product_decay, summed = lax.associative_scan(compose, block_pair, axis=0)
        block_states = product_decay * carry_state[None, :] + summed
        return (block_states[-1], block_states)

    shaped = (
        decays.reshape(length // block_rows, block_rows, columns),
        drives.reshape(length // block_rows, block_rows, columns),
    )
    _, all_states = lax.scan(one_block, initial, shaped)
    return all_states.reshape(length, columns)


def contract(left_side, right_side):
    return lax.dot_general(
        left_side, right_side, (((0,), (0,)), ((), ())), preferred_element_type=jnp.float32
    )


def token_rows(piece):
    return lax.all_gather(piece, "gate", axis=0, tiled=True)


def row_sums(triples):
    running = None
    for left_side, right_side, right_axis in triples:
        product = lax.dot_general(
            left_side,
            right_side,
            (((1,), (right_axis,)), ((), ())),
            preferred_element_type=jnp.float32,
        )
        running = product if running is None else running + product
    return lax.psum_scatter(running, "gate", scatter_dimension=0, tiled=True)


def mixer_fetch(input_weights, output_weights, gate_weights):
    return one_gather(
        (
            input_weights.astype(jnp.bfloat16),
            output_weights.astype(jnp.bfloat16),
            gate_weights.astype(jnp.bfloat16),
        ),
        "seq",
        (1, 1, 2),
    )


def feedforward_fetch(hidden_weights, down_weights):
    return gather_turned(
        (hidden_weights.astype(jnp.bfloat16), down_weights.astype(jnp.bfloat16)), "seq", (1, 1)
    )


def adamw(weight, gradient, first_moment, second_moment, step_rate, decay_rate):
    moment = BETA_ONE * first_moment + (1.0 - BETA_ONE) * gradient
    square = BETA_TWO * second_moment + (1.0 - BETA_TWO) * gradient * gradient
    fix_one = 1.0 - BETA_ONE**STEP
    fix_two = 1.0 - BETA_TWO**STEP
    master = weight - step_rate * (
        moment / fix_one / (jnp.sqrt(square / fix_two) + ADAM_EPS) + decay_rate * weight
    )
    return (moment, square, master)


def on_device(
    tokens,
    cotangent,
    start_state,
    slot_table,
    norm_gains,
    gain_first,
    gain_second,
    block_params,
    block_first,
    block_second,
    input_weights,
    input_first,
    input_second,
    output_weights,
    output_first,
    output_second,
    gate_weights,
    gate_first,
    gate_second,
    hidden_weights,
    hidden_first,
    hidden_second,
    down_weights,
    down_first,
    down_second,
):
    slot_count = slot_table.shape[0]
    columns = slot_count * BLOCK
    ff_local = hidden_weights.shape[2]
    column_mask = jnp.repeat((slot_table >= 0).astype(jnp.float32), BLOCK)
    select = (slot_table[:, None] == jnp.arange(NBLK, dtype=jnp.int32)[None, :]).astype(jnp.float32)
    vectors = jnp.einsum("sb,bkc->ksc", select, block_params, precision=HIGHEST).reshape(
        KERNEL + 4, columns
    )
    values = tokens.astype(jnp.float32)
    input_w, output_w, gate_w = mixer_fetch(input_weights, output_weights, gate_weights)
    normed = scale_norm(values, norm_gains[0]).astype(jnp.bfloat16)
    normed_all = token_rows(normed)
    length = normed_all.shape[0]
    branch_x = jnp.dot(normed_all, input_w[0], preferred_element_type=jnp.float32)
    branch_y = jnp.dot(normed_all, input_w[1], preferred_element_type=jnp.float32)
    filtered = causal_taps(branch_x, vectors[3 : 3 + KERNEL], vectors[3 + KERNEL])
    filtered_low = filtered.astype(jnp.bfloat16).reshape(length, slot_count, BLOCK)
    gate_a = (
        jnp.einsum(
            "lsc,scd->lsd", filtered_low, gate_w[0], preferred_element_type=jnp.float32
        ).reshape(length, columns)
        + vectors[1]
    )
    gate_i = (
        jnp.einsum(
            "lsc,scd->lsd", filtered_low, gate_w[1], preferred_element_type=jnp.float32
        ).reshape(length, columns)
        + vectors[2]
    )
    (decays, drives), gating_pull = jax.vjp(gating, gate_a, gate_i, filtered, vectors[0])
    states = run_recurrence(decays, drives, start_state[0])
    active_y, y_pull = jax.vjp(jax.nn.gelu, branch_y)
    mixed_low = (states * active_y * column_mask).astype(jnp.bfloat16)
    middle = values + row_sums(((mixed_low, output_w, 0),))
    hidden_w, down_w = feedforward_fetch(hidden_weights, down_weights)
    second = scale_norm(middle, norm_gains[1]).astype(jnp.bfloat16)
    second_all = token_rows(second)
    gate_value = jnp.dot(second_all, hidden_w[0], preferred_element_type=jnp.float32)
    up_value = jnp.dot(second_all, hidden_w[1], preferred_element_type=jnp.float32)
    active_gate, gate_pull = jax.vjp(jax.nn.gelu, gate_value)
    hidden = (active_gate * up_value).astype(jnp.bfloat16)
    result = middle + row_sums(((hidden, down_w, 0),))
    layer_output = result.astype(jnp.bfloat16)
    input_w, output_w, gate_w = mixer_fetch(input_weights, output_weights, gate_weights)
    hidden_w, down_w = feedforward_fetch(hidden_weights, down_weights)
    cotangent_all = token_rows(cotangent)
    d_hidden = lax.dot_general(
        cotangent_all, down_w, (((1,), (1,)), ((), ())), preferred_element_type=jnp.float32
    )
    d_gate = gate_pull(d_hidden * up_value)[0].astype(jnp.bfloat16)
    d_up = (d_hidden * active_gate).astype(jnp.bfloat16)
    feed_share = lax.psum_scatter(
        jnp.concatenate(
            [
                contract(second_all, d_gate),
                contract(second_all, d_up),
                contract(cotangent_all, hidden),
            ],
            axis=1,
        ).astype(jnp.bfloat16),
        "seq",
        scatter_dimension=0,
        tiled=True,
    ).astype(jnp.float32)
    hidden_grad = jnp.stack([feed_share[:, :ff_local], feed_share[:, ff_local : 2 * ff_local]])
    down_grad = jnp.transpose(feed_share[:, 2 * ff_local :])
    d_second = row_sums(((d_gate, hidden_w[0], 1), (d_up, hidden_w[1], 1)))
    d_norm_two, gain_two = norm_back(middle, norm_gains[1], d_second)
    d_middle = cotangent.astype(jnp.float32) + d_norm_two
    d_out = d_middle.astype(jnp.bfloat16)
    out_all = token_rows(d_out)
    d_mixed = (
        lax.dot_general(
            out_all, output_w, (((1,), (1,)), ((), ())), preferred_element_type=jnp.float32
        )
        * column_mask
    )
    grad_output = contract(mixed_low, out_all)
    d_states = d_mixed * active_y
    d_y = y_pull(d_mixed * states)[0].astype(jnp.bfloat16)
    next_decay = jnp.concatenate([decays[1:], jnp.zeros((1, columns), jnp.float32)], axis=0)
    carried = jnp.flip(
        run_recurrence(
            jnp.flip(next_decay, 0), jnp.flip(d_states, 0), jnp.zeros((columns,), jnp.float32)
        ),
        0,
    )
    previous = jnp.concatenate([start_state, states[:-1]], axis=0)
    d_gate_a, d_gate_i, d_filtered, d_decay_param = gating_pull((carried * previous, carried))
    d_gate_a_low = d_gate_a.astype(jnp.bfloat16).reshape(length, slot_count, BLOCK)
    d_gate_i_low = d_gate_i.astype(jnp.bfloat16).reshape(length, slot_count, BLOCK)
    grad_gates = jnp.stack(
        [
            jnp.einsum(
                "lsc,lsd->scd", filtered_low, d_gate_a_low, preferred_element_type=jnp.float32
            ),
            jnp.einsum(
                "lsc,lsd->scd", filtered_low, d_gate_i_low, preferred_element_type=jnp.float32
            ),
        ]
    )
    from_gates = jnp.einsum(
        "lsd,scd->lsc", d_gate_a_low, gate_w[0], preferred_element_type=jnp.float32
    ) + jnp.einsum("lsd,scd->lsc", d_gate_i_low, gate_w[1], preferred_element_type=jnp.float32)
    d_filtered = d_filtered + from_gates.reshape(length, columns)
    d_branch, tap_grads, tap_bias_grad = taps_back(branch_x, d_filtered, vectors[3 : 3 + KERNEL])
    d_u = d_branch.astype(jnp.bfloat16)
    grad_input = jnp.stack([contract(normed_all, d_u), contract(normed_all, d_y)])
    d_normed = row_sums(((d_u, input_w[0], 1), (d_y, input_w[1], 1)))
    d_norm_one, gain_one = norm_back(values, norm_gains[0], d_normed)
    tokens_gradient = d_middle + d_norm_one
    vector_grads = jnp.concatenate(
        [
            d_decay_param[None],
            jnp.sum(d_gate_a, axis=0)[None],
            jnp.sum(d_gate_i, axis=0)[None],
            tap_grads,
            tap_bias_grad[None],
        ],
        axis=0,
    )
    block_terms = jnp.einsum(
        "sb,ksc->bkc",
        select,
        vector_grads.reshape(KERNEL + 4, slot_count, BLOCK),
        precision=HIGHEST,
    )
    gain_grad, block_grad = lax.psum(
        (jnp.stack([gain_one, gain_two]), block_terms), ("seq", "gate")
    )
    input_grad, output_grad, gate_grad = tuple(
        (
            part.astype(jnp.float32)
            for part in sum_together(
                (
                    grad_input.astype(jnp.bfloat16),
                    grad_output.astype(jnp.bfloat16),
                    grad_gates.astype(jnp.bfloat16),
                ),
                "seq",
                (1, 1, 2),
            )
        )
    )
    gain_moment, gain_square, gain_master = adamw(
        norm_gains, gain_grad, gain_first, gain_second, SMALL_RATE, 0.0
    )
    block_moment, block_square, block_master = adamw(
        block_params, block_grad, block_first, block_second, VECTOR_RATE, 0.0
    )
    input_moment, input_square, input_master = adamw(
        input_weights, input_grad, input_first, input_second, MATRIX_RATE, MATRIX_DECAY
    )
    output_moment, output_square, output_master = adamw(
        output_weights, output_grad, output_first, output_second, MATRIX_RATE, MATRIX_DECAY
    )
    gate_moment, gate_square, gate_master = adamw(
        gate_weights, gate_grad, gate_first, gate_second, MATRIX_RATE, MATRIX_DECAY
    )
    hidden_moment, hidden_square, hidden_master = adamw(
        hidden_weights, hidden_grad, hidden_first, hidden_second, MATRIX_RATE, MATRIX_DECAY
    )
    down_moment, down_square, down_master = adamw(
        down_weights, down_grad, down_first, down_second, MATRIX_RATE, MATRIX_DECAY
    )
    return (
        layer_output,
        tokens_gradient,
        gain_moment,
        gain_square,
        gain_master,
        block_moment,
        block_square,
        block_master,
        input_moment,
        input_square,
        input_master,
        output_moment,
        output_square,
        output_master,
        gate_moment,
        gate_square,
        gate_master,
        hidden_moment,
        hidden_square,
        hidden_master,
        down_moment,
        down_square,
        down_master,
    )


def solution(mesh):
    placed = (
        P(("seq", "gate"), None),
        P(("seq", "gate"), None),
        P("seq", "gate"),
        P("gate"),
        P(),
        P(),
        P(),
        P(),
        P(),
        P(),
        P(None, "seq", "gate"),
        P(None, "seq", "gate"),
        P(None, "seq", "gate"),
        P("gate", "seq"),
        P("gate", "seq"),
        P("gate", "seq"),
        P(None, "gate", "seq", None),
        P(None, "gate", "seq", None),
        P(None, "gate", "seq", None),
        P(None, "seq", "gate"),
        P(None, "seq", "gate"),
        P(None, "seq", "gate"),
        P("gate", "seq"),
        P("gate", "seq"),
        P("gate", "seq"),
    )
    return jax.shard_map(
        on_device,
        mesh=mesh,
        in_specs=placed,
        out_specs=(
            P(("seq", "gate"), None),
            P(("seq", "gate"), None),
            P(),
            P(),
            P(),
            P(),
            P(),
            P(),
            P(None, "seq", "gate"),
            P(None, "seq", "gate"),
            P(None, "seq", "gate"),
            P("gate", "seq"),
            P("gate", "seq"),
            P("gate", "seq"),
            P(None, "gate", "seq", None),
            P(None, "gate", "seq", None),
            P(None, "gate", "seq", None),
            P(None, "seq", "gate"),
            P(None, "seq", "gate"),
            P(None, "seq", "gate"),
            P("gate", "seq"),
            P("gate", "seq"),
            P("gate", "seq"),
        ),
        check_vma=False,
    )
```

profile of v0, /device:TPU:1, one launch (start us, length us, event | category | flops | bytes accessed | tf_op | source)
XLA Modules:
  0.0 1775.1 jit_solution(11503461128609337097)
XLA Ops:
  14.2 67.0 %all-gather.18.cloned.1.call-done = bf16[3407872]{0:T(1024)(128)(2,1)} async-done(((bf16[212992]{0:T(1024)(128)(2,1)}), bf16[3407872]{0:T(1024)(128)(2,1)}) %all-gather.18.cloned.1.call-update) | async-done | bytes 6815760 | tf_op jit(solution)/shard_map/all_gather | solution.py:31
  81.2 6.6 reshape.310
  95.8 75.8 %all-gather.8.cloned.1.call-done = bf16[1024,2048]{1,0:T(8,128)(2,1)} async-done(((bf16[128,2048]{1,0:T(8,128)(2,1)}), bf16[1024,2048]{1,0:T(8,128)(2,1)}) %all-gather.8.cloned.1.call-update) | async-done | bytes 4194320 | tf_op jit(solution)/shard_map/all_gather | solution.py:150
  171.6 4.6 fusion.122
  176.2 3.3 fusion.104
  189.9 4.2 multiply_exponential_fusion.1
  198.7 44.6 %while.24 = (s32[]{:T(128)}, f32[512]{0:T(512)S(1)}, f32[8,128,512]{2,1,0:T(8,128)}, f32[8,128,512]{2,1,0:T(8,128)}, f32[8,128,512]{2,1,0:T(8,128)}, /*index=5*/s32[]{:T(128)}, f32[]{:T(128)}) while((s32[]{:T(128)}, f32[512]{0:T(512)S(1)}, f32[8,128,512]{2,1,0:T(8,128)}, f32[8,128,512]{2,1,0:T(8,128)}, f32[8,128,512]{2,1,0:T(8,128)}, ...), condition=%wide.region_2.3_spmd, body=%wide.region_1.2_spmd.sunk | while | flops 1022466 | bytes 14915777 | solution.py:139
  245.3 4.0 copy.306
  249.3 3.9 copy.245
  253.2 7.1 multiply_convert_fusion.1
  261.4 5.7 fusion.125
  269.6 166.9 %reduce-scatter.9.cloned.1.call-done = f32[128,2048]{1,0:T(8,128)} async-done(((f32[1024,2048]{1,0:T(8,128)}), f32[128,2048]{1,0:T(8,128)}) %reduce-scatter.9.cloned.1.call-update) | async-done | bytes 1048592 | tf_op jit(solution)/shard_map/reduce_scatter | solution.py:163
  439.5 83.3 %all-gather.12.cloned.1.call-done = bf16[2048,2304]{0,1:T(8,128)(2,1)} async-done(((bf16[128,2304]{0,1:T(8,128)(2,1)}), bf16[2048,2304]{0,1:T(8,128)(2,1)}) %all-gather.12.cloned.1.call-update) | async-done | bytes 9437200 | tf_op jit(solution)/shard_map/all_gather | solution.py:43
  522.8 6.5 split.10
  529.3 9.1 copy.247
  538.5 74.3 %all-gather.10.cloned.1.call-done = bf16[1024,2048]{1,0:T(8,128)(2,1)} async-done(((bf16[128,2048]{1,0:T(8,128)(2,1)}), bf16[1024,2048]{1,0:T(8,128)(2,1)}) %all-gather.10.cloned.1.call-update) | async-done | bytes 4194320 | tf_op jit(solution)/shard_map/all_gather | solution.py:150
  612.7 8.4 fusion.28
  621.2 5.0 fusion.29
  626.2 78.8 %all-gather.14.cloned.1.call-done = bf16[1024,2048]{1,0:T(8,128)(2,1)} async-done(((bf16[128,2048]{1,0:T(8,128)(2,1)}), bf16[1024,2048]{1,0:T(8,128)(2,1)}) %all-gather.14.cloned.1.call-update) | async-done | bytes 4194320 | tf_op jit(solution)/shard_map/all_gather | solution.py:150
  705.0 10.4 fusion.25
  715.5 7.2 fusion.27
  722.7 7.6 convolution_add_fusion.1
  730.3 7.6 fusion.32
  738.0 161.7 %reduce-scatter.13.cloned.1.call-done = f32[128,2048]{1,0:T(8,128)} async-done(((f32[1024,2048]{1,0:T(8,128)}), f32[128,2048]{1,0:T(8,128)}) %reduce-scatter.13.cloned.1.call-update) | async-done | bytes 1048592 | tf_op jit(solution)/shard_map/reduce_scatter | solution.py:163
  901.2 171.1 %reduce-scatter.11.cloned.1.call-done = f32[128,2048]{1,0:T(8,128)} async-done(((f32[1024,2048]{1,0:T(8,128)}), f32[128,2048]{1,0:T(8,128)}) %reduce-scatter.11.cloned.1.call-update) | async-done | bytes 1048592 | tf_op jit(solution)/shard_map/reduce_scatter | solution.py:163
  1072.3 3.6 fusion.103
  1077.6 11.8 rev.10
  1092.5 6.1 fusion.26
  1098.6 3.9 convolution_convert_fusion.1
  1102.5 3.8 convolution_convert_fusion.2
  1106.3 4.2 pad_maximum_fusion.24
  1110.6 12.8 copy.289
  1123.6 44.1 %all-gather.16.cloned.1.call-done = bf16[1024,2048]{1,0:T(8,128)(2,1)} async-done(((bf16[128,2048]{1,0:T(8,128)(2,1)}), bf16[1024,2048]{1,0:T(8,128)(2,1)}) %all-gather.16.cloned.1.call-update) | async-done | bytes 4194320 | tf_op jit(solution)/shard_map/all_gather | solution.py:150
  1167.7 8.9 fusion.47
  1176.6 15.1 rev.11
  1193.8 39.3 %while.25 = (s32[]{:T(128)}, f32[512]{0:T(512)S(1)}, f32[8,128,512]{2,1,0:T(8,128)S(1)}, f32[8,128,512]{2,1,0:T(8,128)}, f32[8,128,512]{2,1,0:T(8,128)}, /*index=5*/s32[]{:T(128)}, f32[]{:T(128)}) while((s32[]{:T(128)}, f32[512]{0:T(512)S(1)}, f32[8,128,512]{2,1,0:T(8,128)S(1)}, f32[8,128,512]{2,1,0:T(8,128)}, f32[8,128,512]{2,1,0:T(8,128)}, ...), condition=%wide.region_9.10_spmd, body=%wide.region_8.9_spmd.sunk | while | flops 1022466 | bytes 14915777 | solution.py:139
  1234.9 17.8 %rev.12 = f32[1024,512]{0,1:T(8,128)} reverse(f32[1024,512]{0,1:T(8,128)} %copy.287), dimensions={0} | reverse | bytes 4194304 | tf_op jit(solution)/shard_map/jit(_flip)/rev | solution.py:303
  1252.8 7.8 fusion.99
  1267.0 6.1 multiply_reduce_fusion
  1292.3 4.4 copy.307
  1296.8 16.8 pad_maximum_fusion.25
  1313.5 6.8 reshape.307
  1320.7 4.5 fusion.127
  1325.2 5.7 convolution_add_fusion
  1345.6 89.5 %all-reduce.61.cloned.1.call-done = f32[10,8,256]{2,1,0:T(8,128)} async-done(((f32[10,8,256]{2,1,0:T(8,128)}), f32[10,8,256]{2,1,0:T(8,128)}) %all-reduce.61.cloned.1.call-update) | async-done | bytes 81936 | tf_op jit(solution)/shard_map/psum | solution.py:349
  1436.8 90.0 %reduce-scatter.17.cloned.1.call-done = bf16[1664,128]{1,0:T(8,128)(2,1)} async-done(((bf16[26624,128]{1,0:T(8,128)(2,1)}), bf16[1664,128]{1,0:T(8,128)(2,1)}) %reduce-scatter.17.cloned.1.call-update) | async-done | bytes 426000 | tf_op jit(solution)/shard_map/reduce_scatter | solution.py:64
  1533.9 164.7 %reduce-scatter.15.cloned.1.call-done = f32[128,2048]{1,0:T(8,128)} async-done(((f32[1024,2048]{1,0:T(8,128)}), f32[128,2048]{1,0:T(8,128)}) %reduce-scatter.15.cloned.1.call-update) | async-done | bytes 1048592 | tf_op jit(solution)/shard_map/reduce_scatter | solution.py:163
  1700.2 65.8 %psum.14 = f32[2,2048]{1,0:T(2,128)S(1)} all-reduce(f32[2,2048]{1,0:T(2,128)S(1)} %pad_maximum_fusion.31), channel_id=1, replica_groups=mesh['seq'=16,'gate'=8] {'seq','gate'}, use_global_device_ids=true, to_apply=%region_14.15 | all-reduce | flops 4096 | bytes 32768 | tf_op jit(solution)/shard_map/psum | solution.py:349
  (2051 shorter events, 176.1 us)
Async XLA Ops:
  7.2 74.0 %all-gather.18.cloned.1.call-start = ((), (), s32[]{:S(2)}) async-start(), calls=%async_computation.17 | async-start | bytes 7241728 | tf_op jit(solution)/shard_map/all_gather | solution.py:31
  11.2 160.4 %all-gather.8.cloned.1.call-start = ((), (), s32[]{:S(2)}) async-start(), calls=%async_computation.6 | async-start | bytes 4718592 | tf_op jit(solution)/shard_map/all_gather | solution.py:150
  12.0 75.8 %copy-start.78 = (f32[128]{0:T(128)}, f32[128]{0:T(128)S(1)}, u32[]{:S(2)}) copy-start(f32[128]{0:T(128)S(1)} %get-tuple-element.408) | copy-start | bytes 1540
  12.0 75.7 %copy-start.51 = (f32[1,2048]{1,0:T(1,128)}, f32[1,2048]{1,0:T(1,128)S(1)}, u32[]{:S(2)}) copy-start(f32[1,2048]{1,0:T(1,128)S(1)} %get-tuple-element.396) | copy-start | bytes 24580
  13.0 423.4 %reduce-scatter.9.cloned.1.call-start = ((), (), s32[]{:S(2)}) async-start(), calls=%async_computation.7 | async-start | bytes 9437184 | tf_op jit(solution)/shard_map/reduce_scatter | solution.py:163
  13.3 74.4 %copy-start.55 = (f32[8,2,256]{2,1,0:T(2,128)}, f32[8,2,256]{2,1,0:T(2,128)S(1)}, u32[]{:S(2)}) copy-start(f32[8,2,256]{2,1,0:T(2,128)S(1)} %convolution_bitcast_fusion) | copy-start | bytes 49156
  13.4 162.8 %copy-start.67 = (f32[1,2,2,128]{3,1,2,0:T(2,128)}, f32[1,2,2,128]{3,1,2,0:T(2,128)S(1)}, u32[]{:S(2)}) copy-start(f32[1,2,2,128]{3,1,2,0:T(2,128)S(1)} %copy.300) | copy-start | bytes 6148
  13.4 162.8 %copy-start.69 = (f32[1,2,2,128]{3,1,2,0:T(2,128)}, f32[1,2,2,128]{3,1,2,0:T(2,128)S(1)}, u32[]{:S(2)}) copy-start(f32[1,2,2,128]{3,1,2,0:T(2,128)S(1)} %copy.299) | copy-start | bytes 6148
  13.4 162.7 %copy-start.71 = (f32[1,2,2,128]{3,1,2,0:T(2,128)}, f32[1,2,2,128]{3,1,2,0:T(2,128)S(1)}, u32[]{:S(2)}) copy-start(f32[1,2,2,128]{3,1,2,0:T(2,128)S(1)} %copy.298) | copy-start | bytes 6148
  13.4 162.7 %copy-start.73 = (f32[1,2,2,128]{3,1,2,0:T(2,128)}, f32[1,2,2,128]{3,1,2,0:T(2,128)S(1)}, u32[]{:S(2)}) copy-start(f32[1,2,2,128]{3,1,2,0:T(2,128)S(1)} %copy.296) | copy-start | bytes 6148
  13.5 175.6 %copy-start.56 = (f32[1,2,2,128]{3,1,2,0:T(2,128)}, f32[1,2,2,128]{3,1,2,0:T(2,128)S(1)}, u32[]{:S(2)}) copy-start(f32[1,2,2,128]{3,1,2,0:T(2,128)S(1)} %copy.302) | copy-start | bytes 6148
  13.5 175.6 %copy-start.64 = (f32[1,2,2,128]{3,1,2,0:T(2,128)}, f32[1,2,2,128]{3,1,2,0:T(2,128)S(1)}, u32[]{:S(2)}) copy-start(f32[1,2,2,128]{3,1,2,0:T(2,128)S(1)} %copy.304) | copy-start | bytes 6148
  14.2 174.9 %copy-start.62 = (f32[512]{0:T(512)}, f32[512]{0:T(512)S(1)}, u32[]{:S(2)}) copy-start(f32[512]{0:T(512)S(1)} %get-tuple-element.406) | copy-start | bytes 6148
  89.0 90.5 %copy-start.29 = (bf16[1,2,16,16,256]{4,3,2,1,0:T(8,128)(2,1)}, bf16[1,2,16,16,256]{4,3,2,1,0:T(8,128)(2,1)S(1)}, u32[]{:S(2)}) copy-start(bf16[1,2,16,16,256]{4,3,2,1,0:T(8,128)(2,1)S(1)} %copy.230) | copy-start | bytes 786436
  95.8 80.4 %copy-start.35 = (bf16[1,16,128,512]{3,2,0,1:T(8,128)(2,1)}, bf16[1,16,128,512]{3,2,0,1:T(8,128)(2,1)S(1)}, u32[]{:S(2)}) copy-start(bf16[1,16,128,512]{3,2,0,1:T(8,128)(2,1)S(1)} %get-tuple-element.387) | copy-start | bytes 6291460
  267.1 255.7 %all-gather.12.cloned.1.call-start = ((), (), s32[]{:S(2)}) async-start(), calls=%async_computation.9 | async-start | bytes 10027008 | tf_op jit(solution)/shard_map/all_gather | solution.py:43
  269.5 343.2 %all-gather.10.cloned.1.call-start = ((), (), s32[]{:S(2)}) async-start(), calls=%async_computation.8 | async-start | bytes 4718592 | tf_op jit(solution)/shard_map/all_gather | solution.py:150
  438.9 266.1 %all-gather.14.cloned.1.call-start = ((), (), s32[]{:S(2)}) async-start(), calls=%async_computation.11 | async-start | bytes 4718592 | tf_op jit(solution)/shard_map/all_gather | solution.py:150
  439.5 460.2 %reduce-scatter.13.cloned.1.call-start = ((), (), s32[]{:S(2)}) async-start(), calls=%async_computation.12 | async-start | bytes 9437184 | tf_op jit(solution)/shard_map/reduce_scatter | solution.py:163
  730.3 342.0 %reduce-scatter.11.cloned.1.call-start = ((), (), s32[]{:S(2)}) async-start(), calls=%async_computation.10 | async-start | bytes 9437184 | tf_op jit(solution)/shard_map/reduce_scatter | solution.py:163
  737.9 429.7 %all-gather.16.cloned.1.call-start = ((), (), s32[]{:S(2)}) async-start(), calls=%async_computation.13 | async-start | bytes 4718592 | tf_op jit(solution)/shard_map/all_gather | solution.py:150
  1075.9 257.6 %reduce-scatter.19.cloned.1.call-start = ((), (), s32[]{:S(2)}) async-start(), calls=%async_computation.18 | async-start | bytes 10027008
  1123.3 44.3 %copy-start.11 = (f32[1024,512]{0,1:T(8,128)S(1)}, f32[1024,512]{0,1:T(8,128)}, u32[]{:S(2)}) copy-start(f32[1024,512]{0,1:T(8,128)} %copy-done.10) | copy-start | bytes 6291460
  1123.4 311.8 %all-reduce.61.cloned.1.call-start = ((), (), s32[]{:S(2)}) async-start(), calls=%async_computation.15 | async-start | bytes 163840 | tf_op jit(solution)/shard_map/psum | solution.py:349
  1234.9 17.9 %copy-start.65 = (f32[1,2,2,128]{3,1,2,0:T(2,128)S(1)}, f32[1,2,2,128]{3,1,2,0:T(2,128)}, u32[]{:S(2)}) copy-start(f32[1,2,2,128]{3,1,2,0:T(2,128)} %copy-done.64) | copy-start | bytes 6148
  1234.9 17.9 %copy-start.66 = (f32[512]{0:T(512)S(1)}, f32[512]{0:T(512)}, u32[]{:S(2)}) copy-start(f32[512]{0:T(512)} %get-tuple-element.405) | copy-start | bytes 6148
  1296.7 230.0 %reduce-scatter.17.cloned.1.call-start = ((), (), s32[]{:S(2)}) async-start(), calls=%async_computation.16 | async-start | bytes 7241728 | tf_op jit(solution)/shard_map/reduce_scatter | solution.py:64
  1320.4 378.2 %reduce-scatter.15.cloned.1.call-start = ((), (), s32[]{:S(2)}) async-start(), calls=%async_computation.14 | async-start | bytes 9437184 | tf_op jit(solution)/shard_map/reduce_scatter | solution.py:163
  1342.3 92.9 %copy-start.45 = (f32[10,8,256]{2,1,0:T(8,128)S(1)}, f32[10,8,256]{2,1,0:T(8,128)}, u32[]{:S(2)}) copy-start(f32[10,8,256]{2,1,0:T(8,128)} %param.36) | copy-start | bytes 245764
  1342.3 92.9 %copy-start.53 = (f32[10,8,256]{2,1,0:T(8,128)S(1)}, f32[10,8,256]{2,1,0:T(8,128)}, u32[]{:S(2)}) copy-start(f32[10,8,256]{2,1,0:T(8,128)} %param.38) | copy-start | bytes 245764
  1342.3 92.9 %copy-start.54 = (f32[10,8,256]{2,1,0:T(8,128)S(1)}, f32[10,8,256]{2,1,0:T(8,128)}, u32[]{:S(2)}) copy-start(f32[10,8,256]{2,1,0:T(8,128)} %param.37) | copy-start | bytes 245764
  1345.6 183.0 %copy-start.48 = (f32[2,2,16,256]{3,2,1,0:T(8,128)S(1)}, f32[2,2,16,256]{3,2,1,0:T(8,128)}, u32[]{:S(2)}) copy-start(f32[2,2,16,256]{3,2,1,0:T(8,128)} %param.45) | copy-start | bytes 196612
  1345.6 183.0 %copy-start.58 = (f32[2,2,16,256]{3,2,1,0:T(8,128)S(1)}, f32[2,2,16,256]{3,2,1,0:T(8,128)}, u32[]{:S(2)}) copy-start(f32[2,2,16,256]{3,2,1,0:T(8,128)} %param.47) | copy-start | bytes 196612
  1345.6 183.0 %copy-start.59 = (f32[2,2,16,256]{3,2,1,0:T(8,128)S(1)}, f32[2,2,16,256]{3,2,1,0:T(8,128)}, u32[]{:S(2)}) copy-start(f32[2,2,16,256]{3,2,1,0:T(8,128)} %param.46) | copy-start | bytes 196612
  1345.6 183.7 %copy-start.40 = (f32[512,128]{1,0:T(8,128)S(1)}, f32[512,128]{1,0:T(8,128)}, u32[]{:S(2)}) copy-start(f32[512,128]{1,0:T(8,128)} %param.42) | copy-start | bytes 786436
  1345.6 183.7 %copy-start.49 = (f32[512,128]{1,0:T(8,128)S(1)}, f32[512,128]{1,0:T(8,128)}, u32[]{:S(2)}) copy-start(f32[512,128]{1,0:T(8,128)} %param.44) | copy-start | bytes 786436
  1345.6 183.7 %copy-start.50 = (f32[512,128]{1,0:T(8,128)S(1)}, f32[512,128]{1,0:T(8,128)}, u32[]{:S(2)}) copy-start(f32[512,128]{1,0:T(8,128)} %param.43) | copy-start | bytes 786436
  1436.7 94.5 %copy-start.33 = (f32[2,128,512]{2,1,0:T(8,128)S(1)}, f32[2,128,512]{2,1,0:T(8,128)}, u32[]{:S(2)}) copy-start(f32[2,128,512]{2,1,0:T(8,128)} %param.39) | copy-start | bytes 1572868
  1436.7 94.5 %copy-start.46 = (f32[2,128,512]{2,1,0:T(8,128)S(1)}, f32[2,128,512]{2,1,0:T(8,128)}, u32[]{:S(2)}) copy-start(f32[2,128,512]{2,1,0:T(8,128)} %param.41) | copy-start | bytes 1572868
  1531.2 167.3 %copy-start.7 = (bf16[128,2048]{1,0:T(8,128)(2,1)S(1)}, bf16[128,2048]{1,0:T(8,128)(2,1)}, u32[]{:S(2)}) copy-start(bf16[128,2048]{1,0:T(8,128)(2,1)} %param.29) | copy-start | bytes 1572868
  1531.2 167.3 %copy-start.52 = (f32[1,2048]{1,0:T(1,128)S(1)}, f32[1,2048]{1,0:T(1,128)}, u32[]{:S(2)}) copy-start(f32[1,2048]{1,0:T(1,128)} %copy-done.51) | copy-start | bytes 24580
  1531.3 167.3 %copy-start.79 = (f32[128]{0:T(128)S(1)}, f32[128]{0:T(128)}, u32[]{:S(2)}) copy-start(f32[128]{0:T(128)} %copy-done.78) | copy-start | bytes 1540
  1531.3 234.7 %copy-start.61 = (f32[2,2048]{1,0:T(2,128)S(1)}, f32[2,2048]{1,0:T(2,128)}, u32[]{:S(2)}) copy-start(f32[2,2048]{1,0:T(2,128)} %param.33) | copy-start | bytes 49156
  1531.3 234.7 %copy-start.75 = (f32[2,2048]{1,0:T(2,128)S(1)}, f32[2,2048]{1,0:T(2,128)}, u32[]{:S(2)}) copy-start(f32[2,2048]{1,0:T(2,128)} %param.35) | copy-start | bytes 49156
  1531.3 234.7 %copy-start.76 = (f32[2,2048]{1,0:T(2,128)S(1)}, f32[2,2048]{1,0:T(2,128)}, u32[]{:S(2)}) copy-start(f32[2,2048]{1,0:T(2,128)} %param.34) | copy-start | bytes 49156
  1531.3 235.4 %copy-start.21 = (f32[128,2048]{1,0:T(8,128)S(1)}, f32[128,2048]{1,0:T(8,128)}, u32[]{:S(2)}) copy-start(f32[128,2048]{1,0:T(8,128)} %get-tuple-element.305) | copy-start | bytes 3145732
  1531.3 235.4 %copy-start.82 = (f32[128]{0:T(128)S(1)}, f32[128]{0:T(128)}, u32[]{:S(2)}) copy-start(f32[128]{0:T(128)} %get-tuple-element.407) | copy-start | bytes 1540
  1698.6 68.1 %copy-start.22 = (f32[128,2048]{1,0:T(8,128)S(1)}, f32[128,2048]{1,0:T(8,128)}, u32[]{:S(2)}) copy-start(f32[128,2048]{1,0:T(8,128)} %reduce-scatter.15.cloned.1.call-done) | copy-start | bytes 3145732
  (64 other events, 296.4 us)
Sparse Core Ops, SparseCore 0:
  11.3 69.8 all-gather.17
  83.4 88.1 all-gather.7
  267.2 169.2 reduce-scatter.8
  439.2 83.5 all-gather.11
  524.9 87.8 all-gather.9
  614.2 90.7 all-gather.13
  730.4 169.2 reduce-scatter.12
  902.1 170.1 reduce-scatter.10
  1076.0 91.6 all-gather.15
  1171.9 106.2 reduce-scatter.18
  1296.8 138.2 all-reduce.60
  1439.2 87.4 reduce-scatter.16
  1529.3 169.2 reduce-scatter.14
where the time goes:
time: 1790 us; the launch traced here: 1780 us
  waiting for transfers between devices  1270 us (71%)
  local copies, waits for them, and re-layouts  207 us (12%)
  matrix products  110 us (6%)
  other arithmetic  98.7 us (6%)
  blocking collectives  65.8 us (4%)
    reduce_scatter x4, waiting for transfers between devices, row_sums(): return lax.psum_scatter(running, 'gate', scatter_dimension=0, tiled=True)  664 us
    all_gather x4, waiting for transfers between devices, token_rows(): return lax.all_gather(piece, 'gate', axis=0, tiled=True)  273 us
    reduce_scatter x1, waiting for transfers between devices, sum_together(): lax.psum_scatter(lines, axis, tiled=True).reshape(-1)  90 us
    psum x1, waiting for transfers between devices, on_device(): lax.psum((jnp.stack([gain_one, gain_two]), block_terms), ('seq', 'gate'))  89.5 us
    all_gather x1, waiting for transfers between devices, gather_turned(): whole = lax.all_gather(both, axis, axis=0, tiled=True)  83.3 us
    all_gather x1, waiting for transfers between devices, one_gather(): lines, at, outs = (lax.all_gather(line, axis), 0, [])  67 us
    psum x1, blocking collectives, on_device(): lax.psum((jnp.stack([gain_one, gain_two]), block_terms), ('seq', 'gate'))  65.8 us
    unnamed x230, local copies, waits for them, and re-layouts  47.5 us
  transfers between devices with their start and end apart: 13, of which 12 were waited for; matrix products, arithmetic and copies ran while one was open for 16% of the time, Pallas kernels for 0%

commit v1 on v0

v1 whole, which is shorter than its diff:
```python
import functools

import jax
import jax.numpy as jnp
from jax import lax
from jax.experimental import pallas as pl
from jax.experimental.pallas import tpu as pltpu
from jax.sharding import PartitionSpec as P

NBLK = 10
BLOCK = 256
KERNEL = 4
STEP = 10

NORM_EPS = 1e-06
BETA_ONE = 0.9
BETA_TWO = 0.999
ADAM_EPS = 1e-08
MATRIX_RATE = 0.02
SMALL_RATE = 0.2
VECTOR_RATE = 0.8
MATRIX_DECAY = 0.1
HIGHEST = lax.Precision.HIGHEST

RING = 4
GROUP = 2 * RING
TILE = 8
LANES = 128
PIECES = 12
VMEM = 56 * 1024 * 1024

BF16 = jnp.bfloat16
F32 = jnp.float32


def move(value, axis, step):
    size = lax.axis_size(axis)
    return lax.ppermute(value, axis, [(k, (k + step) % size) for k in range(size)])


def across(value):
    return move(value, "x", 1)


def up(value):
    return move(value, "z", 1)


def down(value):
    return move(value, "z", -1)


def plus(*terms):
    total = terms[0].astype(F32)
    for term in terms[1:]:
        total = total + term.astype(F32)
    return total


def plus_low(*terms):
    return plus(*terms).astype(BF16)


def after(value, *others):
    return lax.optimization_barrier((value, *others))[0]


def gather(value):
    half = value.shape[0] // 2
    a, b = value[:half], value[half:]
    a_x = across(a)
    below, above = up(value), down(value)
    b_x = across(b)
    ax_below, ax_above = up(a_x), down(a_x)
    far = up(below)
    bx_above, bx_below = across(above[half:]), across(below[half:])
    ax_far = down(ax_above)
    bx_far = across(far[half:])
    return [
        value, a_x, b_x,
        above, ax_above, bx_above,
        far, ax_far, bx_far,
        below, ax_below, bx_below,
    ]


def gather_rows(value, other, h):
    pair = jnp.stack([value, other])
    pair = jnp.where(h == 0, pair, pair[::-1])
    return lax.all_gather(pair, ("y", "c"), axis=0, tiled=False)


def scatter_rows(value):
    return lax.psum_scatter(value, ("y", "c"), scatter_dimension=0, tiled=False)


def halves(part, h):
    mine = lax.dynamic_index_in_dim(part, h, 0, keepdims=False)
    return mine, lax.dynamic_index_in_dim(part, 1 - h, 0, keepdims=False)


def trade(pieces):
    return lax.all_to_all(pieces, ("z", "x"), 0, 0)


def scatter(partial, beside=None):
    pieces = trade(partial.reshape(GROUP, -1, partial.shape[1]))
    if beside is not None:
        pieces, beside = lax.optimization_barrier((pieces, beside))
    return jnp.sum(pieces.astype(F32), axis=0), beside


def scatter_seq(mine, theirs):
    got = move(theirs, "c", 1)

    def block(dh, dy):
        return plus(mine[RING * dh + dy], got[RING * dh + dy])

    far_up = move(block(0, 2).astype(BF16), "y", 1)
    far_down = move(block(1, 2).astype(BF16), "y", -1)
    o_below = move(block(1, 1).astype(BF16), "y", 1)
    above = move(block(0, 3).astype(BF16), "y", -1)
    below = move(plus_low(block(0, 1), far_up), "y", 1)
    o_above = move(plus_low(block(1, 3), far_down), "y", -1)
    return plus(block(0, 0), below, above), plus_low(block(1, 0), o_below, o_above)


def sum_over(value, axes):
    for axis in axes:
        size = lax.axis_size(axis)
        step = 1
        while step < size:
            value = value + lax.ppermute(value, axis, [(k, k ^ step) for k in range(size)])
            step *= 2
    return value


def scale_norm(values, gain):
    return values * lax.rsqrt(jnp.mean(values * values, axis=-1, keepdims=True) + NORM_EPS) * gain


def norm_back(values, gain, d_normed):
    inverse = lax.rsqrt(jnp.mean(values * values, axis=-1, keepdims=True) + NORM_EPS)
    scaled = gain * d_normed
    d_values = inverse * scaled - values * inverse**3 * jnp.mean(
        scaled * values, axis=-1, keepdims=True
    )
    return d_values, inverse


def adamw(weight, gradient, first_moment, second_moment, step_rate, decay_rate):
    moment = BETA_ONE * first_moment + (1.0 - BETA_ONE) * gradient
    square = BETA_TWO * second_moment + (1.0 - BETA_TWO) * gradient * gradient
    fix_one = 1.0 - BETA_ONE**STEP
    fix_two = 1.0 - BETA_TWO**STEP
    master = weight - step_rate * (
        moment / fix_one / (jnp.sqrt(square / fix_two) + ADAM_EPS) + decay_rate * weight
    )
    return (moment, square, master)


GELU_SCALE = 0.7978845608028654
GELU_CUBE = 0.044715


def gelu_pair(y):
    t = jnp.tanh(GELU_SCALE * (y + GELU_CUBE * y * y * y))
    value = 0.5 * y * (1.0 + t)
    slope = 0.5 * (1.0 + t) + 0.5 * y * (1.0 - t * t) * GELU_SCALE * (
        1.0 + 3.0 * GELU_CUBE * y * y
    )
    return value, slope


def gelu(y):
    return 0.5 * y * (1.0 + jnp.tanh(GELU_SCALE * (y + GELU_CUBE * y * y * y)))


def one_minus_exp(v, exp_v):
    series = 1.0 + v * (1.0 / 7.0)
    for k in (6.0, 5.0, 4.0, 3.0, 2.0):
        series = 1.0 + v * (1.0 / k) * series
    return jnp.where(v > -0.5, -v * series, 1.0 - exp_v)


def shift_down(win, k):
    if k == 0:
        return win[TILE:]
    return pltpu.roll(win, k, 0)[TILE:]


def shift_up(win, k):
    return win[k : k + win.shape[0] - TILE]


def dot(left, right, dims):
    return lax.dot_general(left, right, (dims, ((), ())), preferred_element_type=F32)


def forward_gates(win, par_ref, gates):
    filtered = par_ref[7:8, :] + par_ref[3:4, :] * shift_down(win, 0)
    for k in range(1, KERNEL):
        filtered = filtered + par_ref[3 + k : 4 + k, :] * shift_down(win, k)
    low = filtered.astype(BF16)
    gate_a = dot(low, gates[0], ((1,), (0,))) + par_ref[1:2, :]
    gate_i = dot(low, gates[1], ((1,), (0,))) + par_ref[2:3, :]
    return filtered, low, jax.nn.sigmoid(gate_a), jax.nn.sigmoid(gate_i)


def unpack_gates(packed_ref, slot, gates, share):
    rows = share // 8
    for g in range(2):
        for half in range(2):
            for s in range(BLOCK // rows):
                at = pl.multiple_of(s * share + (4 * g + 2 * slot + half) * rows, rows)
                gates[g, s * rows : (s + 1) * rows, half * LANES : (half + 1) * LANES] = packed_ref[
                    pl.ds(at, rows), :
                ]


def fill_window(xs, branch_ref, order, chunk):
    xs[0:TILE, :] = jnp.zeros((TILE, xs.shape[1]), F32)

    @pl.loop(0, GROUP)
    def _(i):
        xs[pl.ds(TILE + i * chunk, chunk), :] = branch_ref[order[i], :, :BLOCK]


def scan_tile(a, b, rows):
    for s in (1, 2, 4):
        keep = rows >= s
        b = b + a * jnp.where(keep, pltpu.roll(b, s, 0), 0.0)
        a = a * jnp.where(keep, pltpu.roll(a, s, 0), 1.0)
    return a, b


def scan_tile_back(a, b, rows):
    for s in (1, 2, 4):
        keep = rows < TILE - s
        b = b + a * jnp.where(keep, pltpu.roll(b, TILE - s, 0), 0.0)
        a = a * jnp.where(keep, pltpu.roll(a, TILE - s, 0), 1.0)
    return a, b


def piece_copies(refs, whole, sems):
    copies, at = [], 0
    for k, ref in enumerate(refs):
        rows = ref.shape[0]
        copies.append(pltpu.make_async_copy(ref, whole.at[pl.ds(at, rows), :], sems.at[k]))
        at += rows
    return copies


def load_pieces(refs, whole, sems):
    copies = piece_copies(refs, whole, sems)
    for copy in copies:
        copy.start()
    for copy in copies:
        copy.wait()


def mix_steps(
    chunk, order, par_ref, branch_ref, gates, mixed_ref, mixed_rows, lanes, states_ref, xs
):
    fill_window(xs, branch_ref, order, chunk)
    rows = lax.broadcasted_iota(jnp.int32, (TILE, BLOCK), 0)

    def step(i, carry):
        at = pl.multiple_of(i * chunk, chunk)
        filtered, _, ra, ri = forward_gates(xs[pl.ds(at, chunk + TILE), :], par_ref, gates)
        log_rate = -8.0 * ra * par_ref[0:1, :]
        decay = jnp.exp(log_rate)
        drive = jnp.sqrt(one_minus_exp(2.0 * log_rate, decay * decay)) * ri * filtered
        tiles = []
        for k in range(chunk // TILE):
            part = slice(k * TILE, (k + 1) * TILE)
            a, b = scan_tile(decay[part], drive[part], rows)
            h = b + a * carry
            tiles.append(h)
            carry = jnp.broadcast_to(h[TILE - 1 : TILE], (TILE, BLOCK))
        states = jnp.concatenate(tiles, axis=0)
        states_ref[pl.ds(at, chunk), :] = states
        y = branch_ref[order[i], :, BLOCK:]
        mixed = (states * gelu(y) * par_ref[9:10, :]).astype(BF16)
        mixed_ref[order[i], :, lanes] = mixed
        mixed_rows[pl.ds(at, chunk), lanes] = mixed
        return carry

    lax.fori_loop(0, GROUP, step, jnp.broadcast_to(par_ref[10:11, :], (TILE, BLOCK)))


def mixer_kernel(chunk, share, order, par_ref, given_ref, *rest):
    pieces, rest = rest[:PIECES], rest[PIECES:]
    branch_ref, states_ref, mixed_ref, part_ref, all_ref, weights_ref = rest[:6]
    whole, weights, mixed_rows, gates, xs, sems, share_sems, out_sems = rest[6:]
    slot, slots = pl.program_id(0), pl.num_programs(0)
    width = slots * BLOCK

    def out_copies():
        return (
            pltpu.make_async_copy(whole, all_ref, out_sems.at[0]),
            pltpu.make_async_copy(weights, weights_ref, out_sems.at[1]),
        )

    @pl.when(slot == 0)
    def _():
        copies = piece_copies(pieces, whole, sems)
        for h in range(2):
            for k in range(GROUP):
                to = pl.ds((h * GROUP + k) * share, share)
                copies.append(
                    pltpu.make_async_copy(
                        given_ref.at[k, h], weights.at[to, :], share_sems.at[h * GROUP + k]
                    )
                )
        for copy in copies:
            copy.start()
        for copy in copies:
            copy.wait()
        for copy in out_copies():
            copy.start()

    @pl.loop(0, 2)
    def _(n):
        lanes = pl.ds(pl.multiple_of(n * BLOCK, BLOCK), BLOCK)
        at = pl.multiple_of((2 * slot + n) * BLOCK, BLOCK)
        product = dot(whole[...], weights[:, pl.ds(at, BLOCK)], ((1,), (0,)))
        branch_ref[:, :, lanes] = product.reshape(GROUP, chunk, BLOCK)

    unpack_gates(weights.at[:, pl.ds(3 * width, LANES)], slot, gates, share)
    lanes = pl.ds(pl.multiple_of(slot * BLOCK, BLOCK), BLOCK)
    mix_steps(
        chunk, order, par_ref, branch_ref, gates, mixed_ref, mixed_rows, lanes, states_ref, xs
    )

    @pl.when(slot == slots - 1)
    def _():
        @pl.loop(0, part_ref.shape[1] // BLOCK)
        def _(n):
            at = pl.multiple_of(n * BLOCK, BLOCK)
            product = dot(
                mixed_rows[...], weights[pl.ds(at, BLOCK), 2 * width : 3 * width], ((1,), (1,))
            )
            part_ref[:, pl.ds(at, BLOCK)] = product.astype(BF16)

        for copy in out_copies():
            copy.wait()


def factor_kernel(
    chunk, share, order, par_ref, packed_ref, branch_ref, states_ref,
    low_ref, decay_ref, open_ref, y_ref, a_ref, i_ref, f_ref, l_ref, gates, xs,
):
    fill_window(xs, branch_ref, order, chunk)
    unpack_gates(packed_ref, pl.program_id(0), gates, share)

    def step(i, before):
        at = pl.multiple_of(i * chunk, chunk)
        here = pl.ds(at, chunk)
        filtered, low, ra, ri = forward_gates(xs[pl.ds(at, chunk + TILE), :], par_ref, gates)
        low_ref[here, :] = low
        log_rate = -8.0 * ra * par_ref[0:1, :]
        decay = jnp.exp(log_rate)
        square = decay * decay
        drop = jnp.sqrt(one_minus_exp(2.0 * log_rate, square))
        decay_ref[here, :] = decay
        states = states_ref[here, :]
        previous = shift_down(jnp.concatenate([before, states], axis=0), 1)
        y = branch_ref[order[i], :, BLOCK:]
        value, slope = gelu_pair(y)
        mask = par_ref[9:10, :]
        open_ref[here, :] = (value * mask).astype(BF16)
        y_ref[here, :] = (states * slope * mask).astype(BF16)
        rate_pull = previous * decay - filtered * ri * square / drop
        pull_a = rate_pull * (-8.0 * par_ref[0:1, :]) * ra * (1.0 - ra)
        a_ref[here, :] = pull_a.astype(BF16)
        l_ref[here, :] = (rate_pull * (8.0 * par_ref[8:9, :]) * ra).astype(BF16)
        i_ref[here, :] = (drop * filtered * ri * (1.0 - ri)).astype(BF16)
        f_ref[here, :] = (drop * ri).astype(BF16)
        return states[chunk - TILE :]

    lax.fori_loop(0, GROUP, step, jnp.broadcast_to(par_ref[10:11, :], (TILE, BLOCK)))


def fold(value):
    return jnp.sum(value.reshape(-1, TILE, value.shape[-1]), axis=0)


def unmix_steps(
    chunk, order, par_ref, branch_ref, gates, d_mixed_ref,
    low_ref, decay_ref, open_ref, y_ref, a_ref, i_ref, f_ref, l_ref,
    d_branch_ref, d_rows, lanes_x, lanes_y, d_gate_ref, d_par_ref, ga, gi, sums,
):
    rows = lax.broadcasted_iota(jnp.int32, (TILE, BLOCK), 0)
    sums[...] = jnp.zeros_like(sums)

    def step(n, carries):
        carry, behind = carries
        i = GROUP - 1 - n
        at = pl.multiple_of(i * chunk, chunk)
        here = pl.ds(at, chunk)
        d_mixed = d_mixed_ref[order[i]]
        d_states = d_mixed * open_ref[here, :].astype(F32)
        d_y = (d_mixed * y_ref[here, :].astype(F32)).astype(BF16)
        d_branch_ref[order[i], :, lanes_y] = d_y
        d_rows[here, lanes_y] = d_y
        decay = decay_ref[here, :].astype(F32)
        pushed = decay * d_states
        tiles = [None] * (chunk // TILE)
        for k in reversed(range(chunk // TILE)):
            part = slice(k * TILE, (k + 1) * TILE)
            a, b = scan_tile_back(decay[part], pushed[part], rows)
            w = b + a * carry
            behind_w = jnp.where(rows < TILE - 1, pltpu.roll(w, TILE - 1, 0), carry)
            tiles[k] = d_states[part] + behind_w
            carry = jnp.broadcast_to(w[0:1], (TILE, BLOCK))
        carried = jnp.concatenate(tiles, axis=0)
        d_a = carried * a_ref[here, :].astype(F32)
        d_i = carried * i_ref[here, :].astype(F32)
        a_low, i_low = d_a.astype(BF16), d_i.astype(BF16)
        ga[here, :] = a_low
        gi[here, :] = i_low
        d_f = (
            carried * f_ref[here, :].astype(F32)
            + dot(a_low, gates[0], ((1,), (1,)))
            + dot(i_low, gates[1], ((1,), (1,)))
        )
        win = jnp.concatenate([d_f, behind], axis=0)
        x = branch_ref[order[i], :, :BLOCK]
        d_u = jnp.zeros((chunk, BLOCK), F32)
        for k in range(KERNEL):
            moved = shift_up(win, k)
            d_u = d_u + par_ref[3 + k : 4 + k, :] * moved
            sums[3 + k] += fold(moved * x)
        d_u = d_u.astype(BF16)
        d_branch_ref[order[i], :, lanes_x] = d_u
        d_rows[here, lanes_x] = d_u
        sums[0] += fold(carried * l_ref[here, :].astype(F32))
        sums[1] += fold(d_a)
        sums[2] += fold(d_i)
        sums[7] += fold(d_f)
        return carry, d_f[:TILE]

    nothing = jnp.zeros((TILE, BLOCK), F32)
    lax.fori_loop(0, GROUP, step, (nothing, nothing))
    d_gate_ref[0, 0] = dot(low_ref[...], ga[...], ((0,), (0,))).astype(BF16)
    d_gate_ref[1, 0] = dot(low_ref[...], gi[...], ((0,), (0,))).astype(BF16)
    for k in range(TILE):
        d_par_ref[k : k + 1, :] = jnp.sum(sums[k], axis=0, keepdims=True)


def unmixer_kernel(
    chunk, share, order, par_ref, packed_ref, weights_ref, output_ref, branch_ref,
    low_ref, decay_ref, open_ref, y_ref, a_ref, i_ref, f_ref, l_ref, *rest,
):
    pieces, rest = rest[:PIECES], rest[PIECES:]
    d_branch_ref, d_gate_ref, d_par_ref, part_ref, all_ref = rest[:5]

    def input_copy():
        lanes = pl.ds(0, input_ref.shape[1])
        return pltpu.make_async_copy(weights_ref.at[:, lanes], input_ref, input_sem)

    whole, input_ref, d_rows, d_mixed, gates, ga, gi, sums, sems, out_sem, input_sem = rest[5:]
    slot, slots = pl.program_id(0), pl.num_programs(0)

    @pl.when(slot == 0)
    def _():
        load_pieces(pieces, whole, sems)
        pltpu.make_async_copy(whole, all_ref, out_sem).start()
        input_copy().start()

    product = dot(whole[...], output_ref[...], ((1,), (0,)))
    d_mixed[...] = product.reshape(GROUP, chunk, BLOCK)

    unpack_gates(packed_ref, slot, gates, share)
    at_x = pl.multiple_of(slot * 2 * BLOCK, 2 * BLOCK)
    at_y = pl.multiple_of(slot * 2 * BLOCK + BLOCK, BLOCK)
    unmix_steps(
        chunk, order, par_ref, branch_ref, gates, d_mixed,
        low_ref, decay_ref, open_ref, y_ref, a_ref, i_ref, f_ref, l_ref,
        d_branch_ref, d_rows, pl.ds(at_x, BLOCK), pl.ds(at_y, BLOCK), d_gate_ref, d_par_ref,
        ga, gi, sums,
    )

    @pl.when(slot == slots - 1)
    def _():
        input_copy().wait()

        @pl.loop(0, part_ref.shape[1] // BLOCK)
        def _(n):
            at = pl.multiple_of(n * BLOCK, BLOCK)
            product = dot(d_rows[...], input_ref[pl.ds(at, BLOCK), :], ((1,), (1,)))
            part_ref[:, pl.ds(at, BLOCK)] = product.astype(BF16)

        pltpu.make_async_copy(whole, all_ref, out_sem).wait()


def in_h_order(block):
    lanes = block.shape[-1]
    return jnp.concatenate([block[:, h].reshape(-1, lanes) for h in range(2)], axis=0)


def pull_kernel(order, given_ref, down_ref, out_ref, all_ref, whole, sems, out_sem):
    step, steps = pl.program_id(0), pl.num_programs(0)
    chunk = given_ref.shape[1]

    @pl.when(step == 0)
    def _():
        copies = []
        for i in range(GROUP):
            to = pl.ds(pl.multiple_of(order[i] * chunk, chunk), chunk)
            copies.append(pltpu.make_async_copy(given_ref.at[i], whole.at[to, :], sems.at[i]))
        for copy in copies:
            copy.start()
        for copy in copies:
            copy.wait()
        pltpu.make_async_copy(whole, all_ref, out_sem).start()

    out_ref[...] = dot(whole[...], in_h_order(down_ref[...]), ((1,), (0,)))

    @pl.when(step == steps - 1)
    def _():
        pltpu.make_async_copy(whole, all_ref, out_sem).wait()


def feed_kernel(*rest):
    chunk_of, feed_ref, d_hidden_ref = rest[:3]
    pieces, rest = rest[3 : 3 + PIECES], rest[3 + PIECES :]
    hidden_ref, d_gate_ref, d_up_ref, part_ref, all_ref = rest[:5]
    whole, weights, d_both, gates, ups, sems, weight_sems, out_sem = rest[5:]
    step, steps = pl.program_id(0), pl.num_programs(0)
    tiles = weights.shape[1] // BLOCK
    rows = whole.shape[0] // GROUP

    share = feed_ref.shape[2]

    def weight_copies():
        for t in range(tiles // 2):
            for lanes in (pl.ds(t * BLOCK, BLOCK), pl.ds((t + tiles // 2) * BLOCK, BLOCK)):
                for h in range(2):
                    for k in range(GROUP):
                        to = pl.ds((h * GROUP + k) * share, share)
                        yield pltpu.make_async_copy(
                            feed_ref.at[k, h, :, lanes], weights.at[to, lanes], weight_sems.at[t]
                        )

    @pl.when(step == 0)
    def _():
        copies = piece_copies(pieces, whole, sems)
        for copy in copies:
            copy.start()
        for copy in weight_copies():
            copy.start()
        for copy in copies:
            copy.wait()
        pltpu.make_async_copy(whole, all_ref, out_sem).start()

    for t in range(tiles // 2):
        @pl.when(step == t)
        def _():
            both = 2 * BLOCK
            pltpu.make_async_copy(
                weights.at[:, pl.ds(0, both)], weights.at[:, pl.ds(0, both)], weight_sems.at[t]
            ).wait()

    at_gate = pl.multiple_of(step * BLOCK, BLOCK)
    at_up = pl.multiple_of((step + tiles // 2) * BLOCK, BLOCK)

    gates[...] = dot(whole[...], weights[:, pl.ds(at_gate, BLOCK)], ((1,), (0,)))
    ups[...] = dot(whole[...], weights[:, pl.ds(at_up, BLOCK)], ((1,), (0,)))

    @pl.loop(0, GROUP)
    def _(m):
        here = pl.ds(pl.multiple_of(m * rows, rows), rows)
        up_value = ups[here, :]
        value, slope = gelu_pair(gates[here, :])
        hidden_ref[here, :] = (value * up_value).astype(BF16)
        d_hidden = d_hidden_ref[here, :]
        d_gate = (d_hidden * up_value * slope).astype(BF16)
        d_up = (d_hidden * value).astype(BF16)
        d_gate_ref[here, :] = d_gate
        d_up_ref[here, :] = d_up
        to = pl.ds(pl.multiple_of(chunk_of[m] * rows, rows), rows)
        d_both[to, pl.ds(at_gate, BLOCK)] = d_gate
        d_both[to, pl.ds(at_up, BLOCK)] = d_up

    @pl.when(step == steps - 1)
    def _():
        @pl.loop(0, part_ref.shape[1] // BLOCK)
        def _(n):
            at = pl.multiple_of(n * BLOCK, BLOCK)
            product = dot(d_both[...], weights[pl.ds(at, BLOCK), :], ((1,), (1,)))
            part_ref[:, pl.ds(at, BLOCK)] = product.astype(BF16)

        pltpu.make_async_copy(whole, all_ref, out_sem).wait()


def down_kernel(order, hidden_ref, down_ref, part_ref, rows_ref):
    chunk = hidden_ref.shape[0] // GROUP

    @pl.when(pl.program_id(0) == 0)
    def _():
        for i in range(GROUP):
            at = pl.multiple_of(order[i] * chunk, chunk)
            rows_ref[i * chunk : (i + 1) * chunk, :] = hidden_ref[pl.ds(at, chunk), :]

    weights = down_ref[...].reshape(BLOCK, down_ref.shape[3])
    part_ref[...] = dot(rows_ref[...], weights, ((1,), (1,))).astype(BF16)


def feed_grad_kernel(second_ref, cotangent_ref, d_gate_ref, d_up_ref, hidden_ref, out_ref):
    ff = hidden_ref.shape[1]
    shape = out_ref.shape[:3] + (ff,)
    left = second_ref[...].T
    for k, ref in enumerate((d_gate_ref, d_up_ref)):
        product = dot(left, ref[...], ((1,), (0,)))
        out_ref[:, :, :, k * ff : (k + 1) * ff] = product.astype(BF16).reshape(shape)
    product = dot(cotangent_ref[...].T, hidden_ref[...], ((1,), (0,)))
    out_ref[:, :, :, 2 * ff :] = product.astype(BF16).reshape(shape)


def split_twins(value, core, mine_ref, theirs_ref, lanes):
    half = value.shape[0] // 2
    top, bottom = value[:half].astype(BF16), value[half:].astype(BF16)
    mine_ref[0, :, lanes] = jnp.where(core == 0, top, bottom)
    theirs_ref[0, :, lanes] = jnp.where(core == 0, bottom, top)


def mixer_grad_kernel(
    place, left_ref, right_ref, out_ref, mixed_ref, weight_ref, d_gate_ref,
    mine_ref, theirs_ref, gain_ref,
):
    core, pair = place[GROUP], place[pl.program_id(0)]
    product = dot(left_ref[...].T, right_ref[...], ((1,), (0,)))
    width = product.shape[1]
    split_twins(product, core, mine_ref, theirs_ref, slice(0, width))
    scaled = product * weight_ref[...].astype(F32)
    folded = scaled[:, :LANES]
    for k in range(1, width // LANES):
        folded = folded + scaled[:, k * LANES : (k + 1) * LANES]
    gain_ref[...] = folded
    product = dot(out_ref[...].T, mixed_ref[...], ((1,), (0,)))
    last = width + product.shape[1]
    split_twins(product, core, mine_ref, theirs_ref, slice(width, last))
    slots = d_gate_ref.shape[1]
    rows = product.shape[0] // 2 // 8
    for g in range(2):
        for j in range(slots):
            for half in range(2):
                at = (4 * g + 2 * j + half) * rows
                lanes = slice(half * LANES, (half + 1) * LANES)
                for ref, twin in ((mine_ref, core), (theirs_ref, 1 - core)):
                    start = pl.multiple_of((2 * pair + twin) * rows, rows)
                    ref[0, at : at + rows, last:] = d_gate_ref[g, j, pl.ds(start, rows), lanes]


def mixer_rows_kernel(input_ref, output_ref, gate_ref, out_ref):
    slots = gate_ref.shape[1]
    rows = gate_ref.shape[2]
    for j in range(slots):
        for k in range(2):
            at = (2 * j + k) * BLOCK
            part = input_ref[k, :, j * BLOCK : (j + 1) * BLOCK]
            out_ref[:, at : at + BLOCK] = part.astype(BF16)
    at = 2 * slots * BLOCK
    columns = slots * BLOCK
    out_ref[:, at : at + columns] = output_ref[...].T.astype(BF16)
    at += columns
    for g in range(2):
        for j in range(slots):
            for half in range(2):
                k = (4 * g + 2 * j + half) * rows
                part = gate_ref[g, j, :, half * LANES : (half + 1) * LANES]
                out_ref[k : k + rows, at:] = part.astype(BF16)


def feed_rows_kernel(hidden_ref, down_ref, out_ref):
    ff = hidden_ref.shape[2]
    for k in range(2):
        out_ref[:, k * ff : (k + 1) * ff] = hidden_ref[k].astype(BF16)
    out_ref[:, 2 * ff :] = down_ref[...].T.astype(BF16)


def mixer_adam_kernel(in_ref, *rest):
    given, made = rest[:9], rest[9:]
    slots, rows = given[6].shape[1], given[6].shape[2]
    for j in range(slots):
        lanes = slice(j * BLOCK, (j + 1) * BLOCK)
        for k in range(2):
            at = (2 * j + k) * BLOCK
            grad = in_ref[:, at : at + BLOCK]
            for ref, value in zip(made[:3], step_of(given[:3], grad, (k, slice(None), lanes))):
                ref[k, :, lanes] = value
        at = 2 * slots * BLOCK + j * BLOCK
        grad = in_ref[:, at : at + BLOCK].T
        for ref, value in zip(made[3:6], step_of(given[3:6], grad, (lanes,))):
            ref[lanes, :] = value
    at = 3 * slots * BLOCK
    for g in range(2):
        for j in range(slots):
            for half in range(2):
                k = (4 * g + 2 * j + half) * rows
                lanes = slice(half * LANES, (half + 1) * LANES)
                grad = in_ref[k : k + rows, at:]
                for ref, value in zip(made[6:], step_of(given[6:], grad, (g, j, slice(None), lanes))):
                    ref[g, j, :, lanes] = value


def feed_adam_kernel(grad_ref, *rest):
    given, made = rest[:6], rest[6:]
    ff = given[0].shape[2]
    for k in range(2):
        for t in range(ff // BLOCK):
            lanes = slice(t * BLOCK, (t + 1) * BLOCK)
            grad = grad_ref[:, k * ff + t * BLOCK : k * ff + (t + 1) * BLOCK].astype(F32)
            for ref, value in zip(made[:3], step_of(given[:3], grad, (k, slice(None), lanes))):
                ref[k, :, lanes] = value
    for t in range(ff // BLOCK):
        lanes = slice(t * BLOCK, (t + 1) * BLOCK)
        grad = grad_ref[:, 2 * ff + t * BLOCK : 2 * ff + (t + 1) * BLOCK].astype(F32).T
        for ref, value in zip(made[3:], step_of(given[3:], grad, (lanes,))):
            ref[lanes, :] = value


def step_of(refs, grad, at):
    return adamw(refs[0][at], grad, refs[1][at], refs[2][at], MATRIX_RATE, MATRIX_DECAY)


def kernel_call(body, name, out_shape, flops=0, moved=0, **options):
    return pl.pallas_call(
        body,
        out_shape=out_shape,
        compiler_params=pltpu.CompilerParams(vmem_limit_bytes=VMEM),
        cost_estimate=pl.CostEstimate(flops=flops, bytes_accessed=moved, transcendentals=0),
        name=name,
        **options,
    )


ANY = pl.BlockSpec(memory_space=pl.ANY)


def all_at(shape):
    return pl.BlockSpec(shape, lambda *_: (0,) * len(shape))


def recurrence_calls(chunk, slots, width, share):
    length, columns = GROUP * chunk, slots * BLOCK
    scalars = pl.BlockSpec(memory_space=pltpu.SMEM)
    par = pl.BlockSpec((16, BLOCK), lambda j: (0, j))
    branch = pl.BlockSpec((GROUP, chunk, 2 * BLOCK), lambda j: (0, 0, j))
    packed = pl.BlockSpec((width, LANES), lambda j: (0, 3 * columns // LANES))
    flat = pl.BlockSpec((length, BLOCK), lambda j: (0, j))
    flat_type = jax.ShapeDtypeStruct((length, columns), F32)
    flat_low = jax.ShapeDtypeStruct((length, columns), BF16)
    window = pltpu.VMEM((length + TILE, BLOCK), F32)
    gates = pltpu.VMEM((2, BLOCK, BLOCK), BF16)
    rows_type = jax.ShapeDtypeStruct((length, width), BF16)
    whole = pltpu.VMEM((length, width), BF16)
    size = length * columns

    mixer = kernel_call(
        functools.partial(mixer_kernel, chunk, share),
        "mix",
        [
            jax.ShapeDtypeStruct((GROUP, chunk, 2 * columns), F32),
            flat_type,
            jax.ShapeDtypeStruct((GROUP, chunk, columns), BF16),
            rows_type,
            rows_type,
            jax.ShapeDtypeStruct((width, 3 * columns + LANES), BF16),
        ],
        flops=6 * length * width * columns + 40 * size,
        moved=4 * length * width + 20 * size,
        grid=(slots,),
        in_specs=[scalars, par] + [ANY] * (1 + PIECES),
        out_specs=[
            branch,
            flat,
            all_at((GROUP, chunk, columns)),
            all_at((length, width)),
            ANY,
            ANY,
        ],
        scratch_shapes=[
            whole,
            pltpu.VMEM((width, 3 * columns + LANES), BF16),
            pltpu.VMEM((length, columns), BF16),
            gates,
            window,
            pltpu.SemaphoreType.DMA((PIECES,)),
            pltpu.SemaphoreType.DMA((16,)),
            pltpu.SemaphoreType.DMA((2,)),
        ],
    )
    factors = kernel_call(
        functools.partial(factor_kernel, chunk, share),
        "factors",
        [flat_low, flat_type] + [flat_low] * 6,
        flops=60 * size,
        moved=44 * size,
        grid=(slots,),
        in_specs=[scalars, par, packed, branch, flat],
        out_specs=[flat] * 8,
        scratch_shapes=[gates, window],
    )
    unmixer = kernel_call(
        functools.partial(unmixer_kernel, chunk, share),
        "unmix",
        [
            jax.ShapeDtypeStruct((GROUP, chunk, 2 * columns), BF16),
            jax.ShapeDtypeStruct((2, slots, BLOCK, BLOCK), BF16),
            jax.ShapeDtypeStruct((TILE, columns), F32),
            rows_type,
            rows_type,
        ],
        flops=6 * length * width * columns + 40 * size,
        moved=4 * length * width + 44 * size,
        grid=(slots,),
        in_specs=[
            scalars,
            par,
            packed,
            ANY,
            pl.BlockSpec((width, BLOCK), lambda j: (0, 2 * slots + j)),
            branch,
        ]
        + [flat] * 8
        + [ANY] * PIECES,
        out_specs=[
            all_at((GROUP, chunk, 2 * columns)),
            pl.BlockSpec((2, 1, BLOCK, BLOCK), lambda j: (0, j, 0, 0)),
            pl.BlockSpec((TILE, BLOCK), lambda j: (0, j)),
            all_at((length, width)),
            ANY,
        ],
        scratch_shapes=[
            whole,
            pltpu.VMEM((width, 2 * columns), BF16),
            pltpu.VMEM((length, 2 * columns), BF16),
            pltpu.VMEM((GROUP, chunk, BLOCK), F32),
            gates,
            pltpu.VMEM((length, BLOCK), BF16),
            pltpu.VMEM((length, BLOCK), BF16),
            pltpu.VMEM((TILE, TILE, BLOCK), F32),
            pltpu.SemaphoreType.DMA((PIECES,)),
            pltpu.SemaphoreType.DMA,
            pltpu.SemaphoreType.DMA,
        ],
    )
    return mixer, factors, unmixer


def feed_calls(length, width, share, ff):
    rows_type = jax.ShapeDtypeStruct((length, width), BF16)
    units = jax.ShapeDtypeStruct((length, ff), BF16)
    whole = pltpu.VMEM((length, width), BF16)
    tiles = ff // BLOCK
    unit = pl.BlockSpec((length, BLOCK), lambda t: (0, t))
    sems = [pltpu.SemaphoreType.DMA((PIECES,)), pltpu.SemaphoreType.DMA]
    work = 2 * length * width * ff
    half = width // (2 * share)
    pull = kernel_call(
        pull_kernel,
        "pull",
        [jax.ShapeDtypeStruct((length, ff), F32), rows_type],
        flops=work,
        moved=8 * length * width,
        grid=(tiles,),
        in_specs=[
            pl.BlockSpec(memory_space=pltpu.SMEM),
            ANY,
            pl.BlockSpec((GROUP, 2, share, BLOCK), lambda t: (0, 0, 0, 2 * tiles + t)),
        ],
        out_specs=[unit, ANY],
        scratch_shapes=[whole] + sems,
    )
    feed = kernel_call(
        feed_kernel,
        "feed",
        [units, units, units, rows_type, rows_type],
        flops=4 * work,
        moved=10 * length * width,
        grid=(tiles,),
        in_specs=[pl.BlockSpec(memory_space=pltpu.SMEM), ANY, unit] + [ANY] * PIECES,
        out_specs=[unit, unit, unit, all_at((length, width)), ANY],
        scratch_shapes=[
            whole,
            pltpu.VMEM((width, 2 * ff), BF16),
            pltpu.VMEM((length, 2 * ff), BF16),
            pltpu.VMEM((length, BLOCK), F32),
            pltpu.VMEM((length, BLOCK), F32),
            sems[0],
            pltpu.SemaphoreType.DMA((tiles,)),
            sems[1],
        ],
    )
    down_call = kernel_call(
        down_kernel,
        "down",
        rows_type,
        flops=work,
        moved=4 * length * width,
        grid=(width // BLOCK,),
        in_specs=[
            pl.BlockSpec(memory_space=pltpu.SMEM),
            all_at((length, ff)),
            pl.BlockSpec(
                (BLOCK // share, 1, share, ff), lambda n: (n % (half // 2), n // (half // 2), 0, 2)
            ),
        ],
        out_specs=pl.BlockSpec((length, BLOCK), lambda n: (0, n)),
        scratch_shapes=[pltpu.VMEM((length, ff), BF16)],
    )
    grads = kernel_call(
        feed_grad_kernel,
        "feed_grads",
        jax.ShapeDtypeStruct((half, 2, share, 3 * ff), BF16),
        flops=3 * work,
        moved=10 * length * width,
        grid=(width // (2 * BLOCK),),
        in_specs=[pl.BlockSpec((length, 2 * BLOCK), lambda n: (0, n))] * 2
        + [all_at((length, ff))] * 3,
        out_specs=pl.BlockSpec(
            (2 * BLOCK // share, 1, share, 3 * ff),
            lambda n: (n % (half // 4), n // (half // 4), 0, 0),
        ),
    )
    return pull, feed, down_call, grads


def mixer_grad_call(length, width, columns, slots):
    pairs = width // BLOCK
    left = pl.BlockSpec((length, BLOCK), lambda r, place: (0, place[r]))
    half = BLOCK // 2

    lanes = 3 * columns + LANES
    return kernel_call(
        mixer_grad_kernel,
        "mixer_grads",
        [jax.ShapeDtypeStruct((pairs, half, lanes), BF16)] * 2
        + [jax.ShapeDtypeStruct((width, LANES), F32)],
        flops=6 * length * width * columns,
        moved=8 * length * width,
        grid_spec=pltpu.PrefetchScalarGridSpec(
            num_scalar_prefetch=1,
            grid=(pairs,),
            in_specs=[
                left,
                all_at((length, 2 * columns)),
                left,
                all_at((length, columns)),
                pl.BlockSpec((BLOCK, 2 * columns), lambda r, place: (place[r], 0)),
                all_at((2, slots, BLOCK, BLOCK)),
            ],
            out_specs=[pl.BlockSpec((1, half, lanes), lambda r, place: (r, 0, 0))] * 2
            + [pl.BlockSpec((BLOCK, LANES), lambda r, place: (place[r], 0))],
        ),
    )


def same(arrays):
    return [jax.ShapeDtypeStruct(a.shape, F32) for a in arrays]


def on_device(
    tokens,
    cotangent,
    start_state,
    slot_table,
    norm_gains,
    gain_first,
    gain_second,
    block_params,
    block_first,
    block_second,
    input_weights,
    input_first,
    input_second,
    output_weights,
    output_first,
    output_second,
    gate_weights,
    gate_first,
    gate_second,
    hidden_weights,
    hidden_first,
    hidden_second,
    down_weights,
    down_first,
    down_second,
):
    slots = slot_table.shape[0]
    columns = slots * BLOCK
    ff = hidden_weights.shape[2]
    chunk, width = tokens.shape
    length = GROUP * chunk
    share = input_weights.shape[1]
    mixer, find_factors, unmixer = recurrence_calls(chunk, slots, width, share)
    pull, feed, push_down, feed_grads = feed_calls(length, width, share, ff)
    mixer_grads = mixer_grad_call(length, width, columns, slots)

    z, x = lax.axis_index("z"), lax.axis_index("x")
    h, y, core = lax.axis_index("h"), lax.axis_index("y"), lax.axis_index("c")
    chunks = jnp.arange(GROUP, dtype=jnp.int32)
    order = 2 * ((chunks // 2 - z + RING) % RING) + ((chunks % 2) ^ x)
    chunk_of = 2 * ((chunks // 2 + z) % RING) + ((chunks % 2) ^ x)

    place = jnp.concatenate(
        [RING * (h ^ (chunks // RING)) + (y + chunks) % RING, core[None]]
    ).astype(jnp.int32)

    mixer_lines = kernel_call(
        mixer_rows_kernel, "mixer_rows", jax.ShapeDtypeStruct((share, 3 * columns + LANES), BF16)
    )(input_weights, output_weights, gate_weights)
    column_mask = jnp.repeat((slot_table >= 0).astype(F32), BLOCK)
    select = (slot_table[:, None] == jnp.arange(NBLK, dtype=jnp.int32)[None, :]).astype(F32)
    vectors = jnp.einsum("sb,bkc->ksc", select, block_params, precision=HIGHEST).reshape(
        KERNEL + 4, columns
    )
    pars = jnp.concatenate(
        [
            jax.nn.softplus(-vectors[:1]),
            vectors[1:],
            jax.nn.sigmoid(-vectors[:1]),
            column_mask[None],
            start_state,
            jnp.zeros((5, columns), F32),
        ],
        axis=0,
    )

    values = tokens.astype(F32)
    normed = gather(scale_norm(values, norm_gains[0]).astype(BF16))
    other, normed[1], normed[3], normed[9] = lax.optimization_barrier(
        (move(mixer_lines, "h", 1), normed[1], normed[3], normed[9])
    )
    given = gather_rows(mixer_lines, other, h)
    hidden_now, *normed = lax.optimization_barrier((hidden_weights, *normed))
    feed_lines = kernel_call(
        feed_rows_kernel, "feed_rows", jax.ShapeDtypeStruct((share, 3 * ff), BF16)
    )(hidden_now, down_weights)
    copies = jnp.broadcast_to(after(cotangent, *normed), (GROUP, chunk, width))
    pars, feed_lines, copies = lax.optimization_barrier((pars, feed_lines, copies))
    cotangents = trade(copies)
    other, given = lax.optimization_barrier((move(feed_lines, "h", 1), given))
    branch, states, mixed, part, normed_all, mixer_w = mixer(order, pars, given, *normed)
    feed_w = gather_rows(feed_lines, other, h)
    added, (factors, (d_hidden, cotangent_all)) = scatter(
        part,
        (
            find_factors(order, pars, mixer_w, branch, states),
            pull(order, cotangents, feed_w),
        ),
    )
    middle = values + added
    second = gather(scale_norm(middle, norm_gains[1]).astype(BF16))
    hidden, d_gate, d_up, part, second_all = feed(chunk_of, feed_w, d_hidden, *second)

    d_second, (feed_grad, lower) = scatter(
        part,
        (
            feed_grads(second_all, cotangent_all, d_gate, d_up, hidden),
            push_down(order, hidden, feed_w),
        ),
    )
    feed_part = scatter_rows(feed_grad)
    d_norm_two, inverse = norm_back(middle, norm_gains[1], d_second)
    gain_two = jnp.sum(d_second * middle * inverse, axis=0)
    d_middle = cotangent.astype(F32) + d_norm_two
    outs = gather(d_middle.astype(BF16))
    lower = trade(after(lower, *outs).reshape(GROUP, chunk, width))

    mixed = mixed.reshape(length, columns)
    d_branch, d_gates, d_vectors, part, out_all = unmixer(
        order, pars, mixer_w, mixer_w, mixer_w, branch, *factors, *outs
    )
    d_branch, feed_part = lax.optimization_barrier(
        (d_branch.reshape(length, 2 * columns), feed_part)
    )
    part, lower = lax.optimization_barrier((part, lower))
    pieces = trade(part.reshape(GROUP, chunk, width))
    mine, theirs, gain_one = mixer_grads(
        place, normed_all, d_branch, out_all, mixed, mixer_w, d_gates
    )
    mixer_share, mixer_other = scatter_seq(mine, theirs)
    feed_share, feed_other = halves(feed_part, h)
    gain_one = jnp.sum(gain_one, axis=1) / norm_gains[0]
    small = jnp.concatenate([gain_one, gain_two, d_vectors.reshape(-1)]).reshape(-1, LANES)
    small = sum_over(small, "cy")
    pieces, mixer_other, feed_other, small = lax.optimization_barrier(
        (pieces, mixer_other, feed_other, small)
    )
    d_normed = jnp.sum(pieces.astype(F32), axis=0)
    mixer_share = plus(mixer_share, move(mixer_other, "h", 1))
    feed_share = plus(feed_share, move(feed_other, "h", 1))
    layer_output = (middle + jnp.sum(lower.astype(F32), axis=0)).astype(BF16)
    d_norm_one, _ = norm_back(values, norm_gains[0], d_normed)
    tokens_gradient = d_middle + d_norm_one

    small = sum_over(small, "h").reshape(-1)
    block_terms = jnp.einsum(
        "sb,ksc->bkc",
        select,
        small[2 * width :].reshape(KERNEL + 4, slots, BLOCK),
        precision=HIGHEST,
    )
    small = sum_over(
        jnp.concatenate([small[: 2 * width], block_terms.reshape(-1)]).reshape(-1, LANES), "xz"
    ).reshape(-1)
    gain_grad = small[: 2 * width].reshape(2, width)
    block_grad = small[2 * width :].reshape(block_params.shape)

    feed_arrays = (
        hidden_weights, hidden_first, hidden_second, down_weights, down_first, down_second
    )
    feed_new = kernel_call(feed_adam_kernel, "feed_adam", same(feed_arrays), moved=1 << 23)(
        feed_share, *feed_arrays
    )
    mixer_arrays = (
        input_weights, input_first, input_second,
        output_weights, output_first, output_second,
        gate_weights, gate_first, gate_second,
    )
    mixer_new = kernel_call(mixer_adam_kernel, "mixer_adam", same(mixer_arrays), moved=1 << 23)(
        mixer_share, *mixer_arrays
    )
    return (
        layer_output,
        tokens_gradient,
        *adamw(norm_gains, gain_grad, gain_first, gain_second, SMALL_RATE, 0.0),
        *adamw(block_params, block_grad, block_first, block_second, VECTOR_RATE, 0.0),
        *mixer_new,
        *feed_new,
    )


def solution(mesh):
    seq, gate = ("h", "y", "c"), ("z", "x")
    split_mesh = jax.sharding.Mesh(mesh.devices.reshape(2, RING, 2, RING, 2), seq + gate)
    rows = P(seq + gate, None)
    split = P(None, seq, gate)
    turned = P(gate, seq)
    blocks = P(None, gate, seq, None)
    weights = (split,) * 3 + (turned,) * 3 + (blocks,) * 3 + (split,) * 3 + (turned,) * 3
    return jax.shard_map(
        on_device,
        mesh=split_mesh,
        in_specs=(rows, rows, P(seq, gate), P(gate)) + (P(),) * 6 + weights,
        out_specs=(rows, rows) + (P(),) * 6 + weights,
        check_vma=False,
    )
```

time: 1790 us -> 535 us (0.30)
  waiting for transfers between devices: 1270 us -> 189 us
  local copies, waits for them, and re-layouts: 207 us -> 9.34 us
  Pallas kernels: 0 us -> 157 us
  starting transfers between devices: 1 us -> 116 us
  matrix products: 110 us -> 0.54 us
  blocking collectives: 65.8 us -> 0 us
  other arithmetic: 98.7 us -> 39.7 us
    reduce_scatter x5 -> x1, waiting for transfers between devices: 754 us -> 0.02 us  [scatter_rows(): return lax.psum_scatter(value, ('y', 'c'), scatter_dimension=0, tiled=False)]
    all_gather x6 -> x2, waiting for transfers between devices: 423 us -> 4.22 us  [gather_rows(): return lax.all_gather(pair, ('y', 'c'), axis=0, tiled=False)]
    pallas_call x0 -> x12, Pallas kernels: none -> 157 us  [the longest x1 27.6 us: on_device(): unmixer(order, pars, mixer_w, mixer_w, mixer_w, branch, *factors, *outs)]
    ppermute x0 -> x51, waiting for transfers between devices: none -> 111 us  [the longest x44 85.5 us: move(): lax.ppermute(value, axis, [(k, (k + step) % size) for k in range(size)])]
    dot_general x25 -> x1, matrix products: 110 us -> 0.33 us  [on_device(): jnp.einsum('sb,ksc->bkc', select, small[2 * width:].reshape(KERNEL + 4, s...]
    ppermute x0 -> x51, starting transfers between devices: none -> 90 us  [the longest x44 75.1 us: move(): lax.ppermute(value, axis, [(k, (k + step) % size) for k in range(size)])]
    psum x1 -> x0, waiting for transfers between devices: 89.5 us -> none  [on_device(): lax.psum((jnp.stack([gain_one, gain_two]), block_terms), ('seq', 'gate'))]
    all_to_all x0 -> x5, waiting for transfers between devices: none -> 73.5 us  [trade(): return lax.all_to_all(pieces, ('z', 'x'), 0, 0)]
  transfers between devices with their start and end apart: 13 -> 59, of which waited for: 12 -> 30; matrix products, arithmetic and copies ran while one was open for 16% -> 7% of each run, Pallas kernels for 0% -> 24%
where the time goes in v1:
time: 535 us; the launch traced here: 526 us
  waiting for transfers between devices  189 us (35%)
  Pallas kernels  157 us (29%)
  starting transfers between devices  116 us (22%)
  other arithmetic  39.7 us (7%)
  between operations  14.9 us (3%)
  local copies, waits for them, and re-layouts  9.34 us (2%)
    ppermute x44, waiting for transfers between devices, move(): lax.ppermute(value, axis, [(k, (k + step) % size) for k in range(size)])  85.5 us
    ppermute x44, starting transfers between devices, move(): lax.ppermute(value, axis, [(k, (k + step) % size) for k in range(size)])  75.1 us
    all_to_all x5, waiting for transfers between devices, trade(): return lax.all_to_all(pieces, ('z', 'x'), 0, 0)  73.5 us
    pallas_call x1, Pallas kernels, on_device(): unmixer(order, pars, mixer_w, mixer_w, mixer_w, branch, *factors, *outs)  27.6 us
    pallas_call x1, Pallas kernels, on_device(): mixer(order, pars, given, *normed)  26.9 us
    pallas_call x1, Pallas kernels, on_device(): feed(chunk_of, feed_w, d_hidden, *second)  26.1 us
    all_to_all x5, starting transfers between devices, trade(): return lax.all_to_all(pieces, ('z', 'x'), 0, 0)  26 us
    ppermute x7, waiting for transfers between devices, sum_over(): lax.ppermute(value, axis, [(k, k ^ step) for k in range(size)])  25.4 us
  transfers between devices with their start and end apart: 59, of which 30 were waited for; matrix products, arithmetic and copies ran while one was open for 7% of the time, Pallas kernels for 24%

profile of v1, /device:TPU:1, one launch (start us, length us, event | category | flops | bytes accessed | tf_op | source)
XLA Modules:
  0.0 526.0 jit_solution(4097839407371775915)
XLA Ops:
  21.0 14.6 %collective-permute-done.1.rest_1_ = bf16[64,2048]{1,0:T(8,128)(2,1)S(1)} collective-permute-done((bf16[64,2048]{1,0:T(8,128)(2,1)S(1)}, bf16[64,2048]{1,0:T(8,128)(2,1)S(1)}, u32[]{:S(2)}, u32[]{:S(2)}) %collective-permute-start.1) | collective-permute-done | bytes 262176 | tf_op jit(solution)/shard_map/ppermute | solution.py:38
  42.9 2.9 collective-permute-done.5.rest_4_
  46.1 6.2 %collective-permute-done.7.rest_6_ = bf16[128,2048]{1,0:T(8,128)(2,1)S(1)} collective-permute-done((bf16[128,2048]{1,0:T(8,128)(2,1)S(1)}, bf16[128,2048]{1,0:T(8,128)(2,1)S(1)}, u32[]{:S(2)}, u32[]{:S(2)}) %collective-permute-start.7) | collective-permute-done | bytes 524320 | tf_op jit(solution)/shard_map/ppermute | solution.py:38
  54.4 3.5 collective-permute-done.10.rest_10_
  67.6 10.2 %collective-permute-done.12 = bf16[128,2304]{1,0:T(8,128)(2,1)S(1)} collective-permute-done((bf16[128,2304]{1,0:T(8,128)(2,1)S(1)}, bf16[128,2304]{1,0:T(8,128)(2,1)S(1)}, u32[]{:S(2)}, u32[]{:S(2)}) %collective-permute-start.12) | collective-permute-done | bytes 589856 | tf_op jit(solution)/shard_map/ppermute | solution.py:38
  77.8 4.2 all-gather.5.cloned.1.call-done
  83.4 5.1 all-to-all-start.1
  89.0 26.9 %mix.1 = (f32[8,128,1024]{2,1,0:T(8,128)}, f32[1024,512]{1,0:T(8,128)}, bf16[8,128,512]{2,1,0:T(8,128)(2,1)}, bf16[1024,2048]{1,0:T(8,128)(2,1)}, bf16[1024,2048...) custom-call(s32[8]{0:T(128)} %fusion.28.order, f32[16,512]{1,0:T(8,128)} %concatenate.12.par_ref, ...), custom_call_target="tpu_custom_call" | custom-call | flops 6463422464 | bytes 18874368 | tf_op jit(solution)/shard_map/mix/pallas_call | solution.py:1047
  116.0 21.7 %all-to-all-done.1.given_ref = bf16[8,128,2048]{2,1,0:T(8,128)(2,1)} async-done(((bf16[8,128,2048]{2,1,0:T(8,128)(2,1)}), bf16[8,128,2048]{2,1,0:T(8,128)(2,1)}, u32[]{:S(2)}, u32[]{:S(2)}) %all-to-all-start.1) | async-done | bytes 4194336 | tf_op jit(solution)/shard_map/all_to_all | solution.py:103
  137.6 4.6 all-to-all-start
  142.2 14.3 %factors.1 = (bf16[1024,512]{1,0:T(8,128)(2,1)}, f32[1024,512]{1,0:T(8,128)}, bf16[1024,512]{1,0:T(8,128)(2,1)}, bf16[1024,512]{1,0:T(8,128)(2,1)}, bf16[1024,51...) custom-call(s32[8]{0:T(128)} %fusion.28.order, ...), custom_call_target="tpu_custom_call" | custom-call | flops 31457280 | bytes 23068672 | tf_op jit(solution)/shard_map/factors/pallas_call | solution.py:1052
  156.6 9.2 %pull.1 = (f32[1024,768]{1,0:T(8,128)}, bf16[1024,2048]{1,0:T(8,128)(2,1)}) custom-call(s32[8]{0:T(128)} %fusion.28.order, bf16[8,128,2048]{2,1,0:T(8,128)(2,1)} %all-to-all-done.1.given_ref, bf16[8,2,128,2304]{3,2,1,0:T(8,128)(2,1)} %bitcast.90), custom_call_target="tpu_custom_call" | custom-call | flops 3221225472 | bytes 16777216 | tf_op jit(solution)/shard_map/pull/pallas_call | solution.py:1053
  165.8 24.5 %all-to-all-done = bf16[8,128,2048]{2,1,0:T(8,128)(2,1)} async-done(((bf16[8,128,2048]{2,1,0:T(8,128)(2,1)}), bf16[8,128,2048]{2,1,0:T(8,128)(2,1)}, u32[]{:S(2)}, u32[]{:S(2)}) %all-to-all-start) | async-done | bytes 4194336 | tf_op jit(solution)/shard_map/all_to_all | solution.py:103
  190.3 3.0 convert_reduce_fusion.3
  197.5 8.9 %collective-permute-done.18.rest_12_ = bf16[128,2048]{1,0:T(8,128)(2,1)S(1)} collective-permute-done((bf16[128,2048]{1,0:T(8,128)(2,1)S(1)}, bf16[128,2048]{1,0:T(8,128)(2,1)S(1)}, u32[]{:S(2)}, u32[]{:S(2)}) %collective-permute-start.18) | collective-permute-done | bytes 524320 | tf_op jit(solution)/shard_map/ppermute | solution.py:38
  212.4 3.5 collective-permute-start.23
  217.8 4.6 collective-permute-start.21
  224.3 5.6 %collective-permute-done.21.rest_11_ = bf16[64,2048]{1,0:T(8,128)(2,1)S(1)} collective-permute-done((bf16[64,2048]{1,0:T(8,128)(2,1)S(1)}, bf16[64,2048]{1,0:T(8,128)(2,1)S(1)}, u32[]{:S(2)}, u32[]{:S(2)}) %collective-permute-start.21) | collective-permute-done | bytes 262176 | tf_op jit(solution)/shard_map/ppermute | solution.py:38
  230.7 26.1 %feed.1 = (bf16[1024,768]{1,0:T(8,128)(2,1)}, bf16[1024,768]{1,0:T(8,128)(2,1)}, bf16[1024,768]{1,0:T(8,128)(2,1)}, bf16[1024,2048]{1,0:T(8,128)(2,1)}, bf16[1024,2048]{1,0:T(8,128)(2,1)}) custom-call(s32[8]{0:T(128)} %fusion.30.rest_0_, bf16[8,2,128,2304]{3,2,1,0:T(8,128)(2,1)} %bitcast.91, f32[1024,768]{1,0:T(8,128)} %get-tuple-element.159.rest_2_, ...), custom_call_target="tpu_custom_call" | custom-call | flops 12884901888 | bytes 20971520 | tf_op jit(solution)/shard_map/feed/pallas_call | solution.py:1058
  256.8 5.7 %all-to-all-start.2 = ((bf16[8,128,2048]{2,1,0:T(8,128)(2,1)}), bf16[8,128,2048]{2,1,0:T(8,128)(2,1)}, u32[]{:S(2)}, u32[]{:S(2)}) async-start(bf16[8,128,2048]{2,1,0:T(8,128)(2,1)} %bitcast.96), calls=%async_computation.2 | async-start | bytes 8388608 | tf_op jit(solution)/shard_map/all_to_all | solution.py:103
  262.6 9.4 %down.1 = bf16[1024,2048]{1,0:T(8,128)(2,1)} custom-call(s32[8]{0:T(128)} %fusion.28.order, bf16[1024,768]{1,0:T(8,128)(2,1)} %get-tuple-element.165.hidden_ref, bf16[8,2,128,2304]{3,2,1,0:T(8,128)(2,1)} %bitcast.92), custom_call_target="tpu_custom_call" | custom-call | flops 3221225472 | bytes 8388608 | tf_op jit(solution)/shard_map/down/pallas_call | solution.py:1064
  271.9 15.2 %feed_grads.1 = bf16[8,2,128,2304]{3,2,1,0:T(8,128)(2,1)} custom-call(bf16[1024,2048]{1,0:T(8,128)(2,1)} %get-tuple-element.161.second_ref, bf16[1024,2048]{1,0:T(8,128)(2,1)} %get-tuple-element.162.cotangent_ref, bf16[1024,768]{1,0:T(8,128)(2,1)} %get-tuple-element.163.d_gate_ref, bf16[1024,768]{1,0:T(8,128)(2,1)} %get-tuple-element.164.d_up_ref, ...), custom_call_target="tpu_custom_call" | custom-call | flops 9663676416 | bytes 20971520 | tf_op jit(solution)/shard_map/feed_grads/pallas_call | solution.py:1063
  287.1 21.4 %all-to-all-done.2 = bf16[8,128,2048]{2,1,0:T(8,128)(2,1)} async-done(((bf16[8,128,2048]{2,1,0:T(8,128)(2,1)}), bf16[8,128,2048]{2,1,0:T(8,128)(2,1)}, u32[]{:S(2)}, u32[]{:S(2)}) %all-to-all-start.2) | async-done | bytes 4194336 | tf_op jit(solution)/shard_map/all_to_all | solution.py:103
  308.6 3.0 convert_reduce_fusion.2
  315.2 2.8 collective-permute-start.24
  318.0 4.8 collective-permute-done.29.rest_9_
  322.8 11.3 %collective-permute-start.27 = (bf16[64,2048]{1,0:T(8,128)(2,1)S(1)}, bf16[64,2048]{1,0:T(8,128)(2,1)}, u32[]{:S(2)}, u32[]{:S(2)}) collective-permute-start(bf16[64,2048]{1,0:T(8,128)(2,1)S(1)} %collective-permute-done.24.rest_1_), channel_id=1, source_target_pairs={{0,6},{2,0},{4,2},{6,4},{1,7},{3,1},{5,3},{7,5},{8,14},{10,8},{12,... | collective-permute-start | bytes 786440 | tf_op jit(solution)/shard_map/ppermute | solution.py:38
  334.1 5.7 %collective-permute-start.25 = (bf16[64,2048]{1,0:T(8,128)(2,1)S(1)}, bf16[64,2048]{1,0:T(8,128)(2,1)}, u32[]{:S(2)}, u32[]{:S(2)}) collective-permute-start(bf16[64,2048]{1,0:T(8,128)(2,1)S(1)} %get-tuple-element.221), channel_id=1, source_target_pairs={{0,1},{1,0},{2,3},{3,2},{4,5},{5,4},{6,7},{7,6},{8,9},{9,8},{10,11... | collective-permute-start | bytes 786440 | tf_op jit(solution)/shard_map/ppermute | solution.py:38
  341.8 3.4 collective-permute-start.34
  348.1 3.1 collective-permute-done.31.rest_7_
  351.2 4.2 collective-permute-done.34.rest_11_
  355.4 5.6 %collective-permute-done.32.rest_8_ = bf16[64,2048]{1,0:T(8,128)(2,1)} collective-permute-done((bf16[64,2048]{1,0:T(8,128)(2,1)}, bf16[64,2048]{1,0:T(8,128)(2,1)}, u32[]{:S(2)}, u32[]{:S(2)}) %collective-permute-start.32) | collective-permute-done | bytes 262176 | tf_op jit(solution)/shard_map/ppermute | solution.py:38
  361.0 4.6 all-to-all-start.3
  365.6 27.6 %unmix.1 = (bf16[8,128,1024]{2,1,0:T(8,128)(2,1)}, bf16[2,2,256,256]{3,2,1,0:T(8,128)(2,1)}, f32[8,512]{1,0:T(8,128)}, bf16[1024,2048]{1,0:T(8,128)(2,1)}, bf16[1024,2048]{1,0:T(8,128)(2,1)}) custom-call(s32[8]{0:T(128)} %fusion.28.order, f32[16,512]{1,0:T(8,128)} %concatenate.12.par_ref, ...), custom_call_target="tpu_custom_call" | custom-call | flops 6463422464 | bytes 31457280 | tf_op jit(solution)/shard_map/unmix/pallas_call | solution.py:1075
  393.2 15.2 %mixer_grads.1 = (bf16[8,128,1664]{2,1,0:T(8,128)(2,1)}, bf16[8,128,1664]{2,1,0:T(8,128)(2,1)}, f32[2048,128]{1,0:T(8,128)}) custom-call(s32[9]{0:T(128)} %pad_add_fusion.place, bf16[1024,2048]{1,0:T(8,128)(2,1)} %get-tuple-element.172.left_ref, bf16[1024,1024]{1,0:T(8,128)(2,1)} %bitcast.123, bf16[1024,2048]{1,0:T(8,128)(2,1)} %get-tuple-element.176.out_ref, ...), custom_call_target="tpu_custom_call" | custom-call | flops 6442450944 | bytes 16777216 | tf_op jit(solution)/shard_map/mixer_grads/pallas_call | solution.py:1083
  408.4 3.0 collective-permute-start.35
  411.9 6.1 %all-to-all-start.4 = ((bf16[8,128,2048]{2,1,0:T(8,128)(2,1)}), bf16[8,128,2048]{2,1,0:T(8,128)(2,1)}, u32[]{:S(2)}, u32[]{:S(2)}) async-start(bf16[8,128,2048]{2,1,0:T(8,128)(2,1)} %bitcast.94), calls=%async_computation.4 | async-start | bytes 8388608 | tf_op jit(solution)/shard_map/all_to_all | solution.py:103
  418.0 4.0 convert_reduce_fusion.1
  426.4 3.1 fusion.15
  433.4 7.5 %collective-permute-done.37 = bf16[128,1664]{1,0:T(8,128)(2,1)S(1)} collective-permute-done((bf16[128,1664]{1,0:T(8,128)(2,1)S(1)}, bf16[128,1664]{1,0:T(8,128)(2,1)S(1)}, u32[]{:S(2)}, u32[]{:S(2)}) %collective-permute-start.37) | collective-permute-done | bytes 426016 | tf_op jit(solution)/shard_map/ppermute | solution.py:38
  447.3 4.0 collective-permute-done.41
  451.3 6.3 %collective-permute-start.48 = (bf16[128,1664]{1,0:T(8,128)(2,1)}, bf16[128,1664]{1,0:T(8,128)(2,1)}, u32[]{:S(2)}, u32[]{:S(2)}) collective-permute-start(bf16[128,1664]{1,0:T(8,128)(2,1)} %get-tuple-element.218), channel_id=1, source_target_pairs={{0,48},{16,0},{32,16},{48,32},{1,49},{17,1},{33,17},{49,33},{2,50}... | collective-permute-start | bytes 1277960 | tf_op jit(solution)/shard_map/ppermute | solution.py:38
  459.7 5.3 %all-to-all-done.4 = bf16[8,128,2048]{2,1,0:T(8,128)(2,1)} async-done(((bf16[8,128,2048]{2,1,0:T(8,128)(2,1)}), bf16[8,128,2048]{2,1,0:T(8,128)(2,1)}, u32[]{:S(2)}, u32[]{:S(2)}) %all-to-all-start.4) | async-done | bytes 4194336 | tf_op jit(solution)/shard_map/all_to_all | solution.py:103
  470.6 3.0 convert_reduce_fusion
  473.6 14.6 %collective-permute-done.42 = f32[64,128]{1,0:T(8,128)S(1)} collective-permute-done((f32[64,128]{1,0:T(8,128)S(1)}, f32[64,128]{1,0:T(8,128)S(1)}, u32[]{:S(2)}, u32[]{:S(2)}) %collective-permute-start.42) | collective-permute-done | bytes 32800 | tf_op jit(solution)/shard_map/ppermute | solution.py:133
  492.3 5.5 %collective-permute-start.44 = (f32[192,128]{1,0:T(8,128)S(1)}, f32[192,128]{1,0:T(8,128)S(1)}, u32[]{:S(2)}, u32[]{:S(2)}) collective-permute-start(f32[192,128]{1,0:T(8,128)S(1)} %fusion.37), channel_id=1, source_target_pairs={{0,2},{2,0},{4,6},{6,4},{1,3},{3,1},{5,7},{7,5},{8,10},{10,8},{12,... | collective-permute-start | bytes 294920 | tf_op jit(solution)/shard_map/ppermute | solution.py:133
  509.6 3.7 mixer_adam.1
  514.5 4.7 feed_adam.1
  (259 shorter events, 97.5 us)
Async XLA Ops:
  7.2 74.9 %all-gather.5.cloned.1.call-start = ((), (), s32[]{:S(2)}) async-start(), calls=%async_computation.7 | async-start | bytes 7667712 | tf_op jit(solution)/shard_map/all_gather | solution.py:90
  11.1 24.5 %collective-permute-start.3 = (bf16[128,2048]{1,0:T(8,128)(2,1)S(1)}, bf16[128,2048]{1,0:T(8,128)(2,1)S(1)}, u32[]{:S(2)}, u32[]{:S(2)}) collective-permute-start(bf16[128,2048]{1,0:T(8,128)(2,1)S(1)} %fusion.2.rest_0_), channel_id=1, source_target_pairs={{0,2},{2,4},{4,6},{6,0},{1,3},{3,5},{5,7},{7,1},{8,10},{10,12},{12... | collective-permute-start | bytes 1572872 | tf_op jit(solution)/shard_map/ppermute | solution.py:38
  13.6 22.0 %collective-permute-start.2 = (bf16[128,2048]{1,0:T(8,128)(2,1)S(1)}, bf16[128,2048]{1,0:T(8,128)(2,1)S(1)}, u32[]{:S(2)}, u32[]{:S(2)}) collective-permute-start(bf16[128,2048]{1,0:T(8,128)(2,1)S(1)} %fusion.2.rest_0_), channel_id=1, source_target_pairs={{0,6},{2,0},{4,2},{6,4},{1,7},{3,1},{5,3},{7,5},{8,14},{10,8},{12,... | collective-permute-start | bytes 1572872 | tf_op jit(solution)/shard_map/ppermute | solution.py:38
  17.8 17.8 %collective-permute-start = (bf16[128,1664]{1,0:T(8,128)(2,1)}, bf16[128,1664]{1,0:T(8,128)(2,1)S(1)}, u32[]{:S(2)}, u32[]{:S(2)}) collective-permute-start(bf16[128,1664]{1,0:T(8,128)(2,1)} %mixer_rows.1), channel_id=1, source_target_pairs={{0,64},{64,0},{1,65},{65,1},{2,66},{66,2},{3,67},{67,3},{4,68},{68... | collective-permute-start | bytes 1277960 | tf_op jit(solution)/shard_map/ppermute | solution.py:38
  20.6 15.0 %collective-permute-start.1 = (bf16[64,2048]{1,0:T(8,128)(2,1)S(1)}, bf16[64,2048]{1,0:T(8,128)(2,1)S(1)}, u32[]{:S(2)}, u32[]{:S(2)}) collective-permute-start(bf16[64,2048]{1,0:T(8,128)(2,1)S(1)} %get-tuple-element.226), channel_id=1, source_target_pairs={{0,1},{1,0},{2,3},{3,2},{4,5},{5,4},{6,7},{7,6},{8,9},{9,8},{10,11... | collective-permute-start | bytes 786440 | tf_op jit(solution)/shard_map/ppermute | solution.py:38
  38.2 118.4 %all-gather.7.cloned.1.call-start = ((), (), s32[]{:S(2)}) async-start(), calls=%async_computation.8 | async-start | bytes 10616832 | tf_op jit(solution)/shard_map/all_gather | solution.py:90
  38.2 14.0 %collective-permute-start.4 = (bf16[64,2048]{1,0:T(8,128)(2,1)S(1)}, bf16[64,2048]{1,0:T(8,128)(2,1)S(1)}, u32[]{:S(2)}, u32[]{:S(2)}) collective-permute-start(bf16[64,2048]{1,0:T(8,128)(2,1)S(1)} %get-tuple-element.225), channel_id=1, source_target_pairs={{0,1},{1,0},{2,3},{3,2},{4,5},{5,4},{6,7},{7,6},{8,9},{9,8},{10,11... | collective-permute-start | bytes 786440 | tf_op jit(solution)/shard_map/ppermute | solution.py:38
  39.7 12.6 %collective-permute-start.7 = (bf16[128,2048]{1,0:T(8,128)(2,1)S(1)}, bf16[128,2048]{1,0:T(8,128)(2,1)S(1)}, u32[]{:S(2)}, u32[]{:S(2)}) collective-permute-start(bf16[128,2048]{1,0:T(8,128)(2,1)S(1)} %collective-permute-done.3.rest_9_), channel_id=1, source_target_pairs={{0,2},{2,4},{4,6},{6,0},{1,3},{3,5},{5,7},{7,1},{8,10},{10,12},{12... | collective-permute-start | bytes 1572872 | tf_op jit(solution)/shard_map/ppermute | solution.py:38
  42.4 15.5 %collective-permute-start.10 = (bf16[64,2048]{1,0:T(8,128)(2,1)S(1)}, bf16[64,2048]{1,0:T(8,128)(2,1)}, u32[]{:S(2)}, u32[]{:S(2)}) collective-permute-start(bf16[64,2048]{1,0:T(8,128)(2,1)S(1)} %collective-permute-done.1.rest_1_), channel_id=1, source_target_pairs={{0,2},{2,4},{4,6},{6,0},{1,3},{3,5},{5,7},{7,1},{8,10},{10,12},{12... | collective-permute-start | bytes 786440 | tf_op jit(solution)/shard_map/ppermute | solution.py:38
  42.5 15.6 %collective-permute-start.11 = (bf16[64,2048]{1,0:T(8,128)(2,1)S(1)}, bf16[64,2048]{1,0:T(8,128)(2,1)}, u32[]{:S(2)}, u32[]{:S(2)}) collective-permute-start(bf16[64,2048]{1,0:T(8,128)(2,1)S(1)} %slice.178), channel_id=1, source_target_pairs={{0,1},{1,0},{2,3},{3,2},{4,5},{5,4},{6,7},{7,6},{8,9},{9,8},{10,11... | collective-permute-start | bytes 786440 | tf_op jit(solution)/shard_map/ppermute | solution.py:38
  45.8 12.3 %collective-permute-start.6 = (bf16[64,2048]{1,0:T(8,128)(2,1)S(1)}, bf16[64,2048]{1,0:T(8,128)(2,1)S(1)}, u32[]{:S(2)}, u32[]{:S(2)}) collective-permute-start(bf16[64,2048]{1,0:T(8,128)(2,1)S(1)} %slice.176), channel_id=1, source_target_pairs={{0,1},{1,0},{2,3},{3,2},{4,5},{5,4},{6,7},{7,6},{8,9},{9,8},{10,11... | collective-permute-start | bytes 786440 | tf_op jit(solution)/shard_map/ppermute | solution.py:38
  52.3 8.5 %collective-permute-start.9 = (bf16[64,2048]{1,0:T(8,128)(2,1)S(1)}, bf16[64,2048]{1,0:T(8,128)(2,1)S(1)}, u32[]{:S(2)}, u32[]{:S(2)}) collective-permute-start(bf16[64,2048]{1,0:T(8,128)(2,1)S(1)} %slice.177), channel_id=1, source_target_pairs={{0,1},{1,0},{2,3},{3,2},{4,5},{5,4},{6,7},{7,6},{8,9},{9,8},{10,11... | collective-permute-start | bytes 786440 | tf_op jit(solution)/shard_map/ppermute | solution.py:38
  65.6 12.3 %collective-permute-start.12 = (bf16[128,2304]{1,0:T(8,128)(2,1)S(1)}, bf16[128,2304]{1,0:T(8,128)(2,1)S(1)}, u32[]{:S(2)}, u32[]{:S(2)}) collective-permute-start(bf16[128,2304]{1,0:T(8,128)(2,1)S(1)} %copy-done.3), channel_id=1, source_target_pairs={{0,64},{64,0},{1,65},{65,1},{2,66},{66,2},{3,67},{67,3},{4,68},{68... | collective-permute-start | bytes 1769480 | tf_op jit(solution)/shard_map/ppermute | solution.py:38
  83.4 54.2 %all-to-all-start.1 = ((bf16[8,128,2048]{2,1,0:T(8,128)(2,1)}), bf16[8,128,2048]{2,1,0:T(8,128)(2,1)}, u32[]{:S(2)}, u32[]{:S(2)}) async-start(bf16[8,128,2048]{2,1,0:T(8,128)(2,1)} %broadcast_in_dim.10), calls=%async_computation.1 | async-start | bytes 8388608 | tf_op jit(solution)/shard_map/all_to_all | solution.py:103
  137.6 52.7 %all-to-all-start = ((bf16[8,128,2048]{2,1,0:T(8,128)(2,1)}), bf16[8,128,2048]{2,1,0:T(8,128)(2,1)}, u32[]{:S(2)}, u32[]{:S(2)}) async-start(bf16[8,128,2048]{2,1,0:T(8,128)(2,1)} %bitcast.95), calls=%async_computation | async-start | bytes 8388608 | tf_op jit(solution)/shard_map/all_to_all | solution.py:103
  193.7 12.7 %collective-permute-start.18 = (bf16[128,2048]{1,0:T(8,128)(2,1)S(1)}, bf16[128,2048]{1,0:T(8,128)(2,1)S(1)}, u32[]{:S(2)}, u32[]{:S(2)}) collective-permute-start(bf16[128,2048]{1,0:T(8,128)(2,1)S(1)} %multiply_convert_fusion.rest_3_), channel_id=1, source_target_pairs={{0,2},{2,4},{4,6},{6,0},{1,3},{3,5},{5,7},{7,1},{8,10},{10,12},{12... | collective-permute-start | bytes 1572872 | tf_op jit(solution)/shard_map/ppermute | solution.py:38
  194.1 17.1 %collective-permute-start.15 = (bf16[128,2048]{1,0:T(8,128)(2,1)S(1)}, bf16[128,2048]{1,0:T(8,128)(2,1)S(1)}, u32[]{:S(2)}, u32[]{:S(2)}) collective-permute-start(bf16[128,2048]{1,0:T(8,128)(2,1)S(1)} %multiply_convert_fusion.rest_3_), channel_id=1, source_target_pairs={{0,6},{2,0},{4,2},{6,4},{1,7},{3,1},{5,3},{7,5},{8,14},{10,8},{12,... | collective-permute-start | bytes 1572872 | tf_op jit(solution)/shard_map/ppermute | solution.py:38
  196.8 9.6 %collective-permute-start.13 = (bf16[64,2048]{1,0:T(8,128)(2,1)S(1)}, bf16[64,2048]{1,0:T(8,128)(2,1)S(1)}, u32[]{:S(2)}, u32[]{:S(2)}) collective-permute-start(bf16[64,2048]{1,0:T(8,128)(2,1)S(1)} %get-tuple-element.224), channel_id=1, source_target_pairs={{0,1},{1,0},{2,3},{3,2},{4,5},{5,4},{6,7},{7,6},{8,9},{9,8},{10,11... | collective-permute-start | bytes 786440 | tf_op jit(solution)/shard_map/ppermute | solution.py:38
  206.4 11.4 %collective-permute-start.19 = (bf16[128,2048]{1,0:T(8,128)(2,1)S(1)}, bf16[128,2048]{1,0:T(8,128)(2,1)S(1)}, u32[]{:S(2)}, u32[]{:S(2)}) collective-permute-start(bf16[128,2048]{1,0:T(8,128)(2,1)S(1)} %collective-permute-done.18.rest_12_), channel_id=1, source_target_pairs={{0,2},{2,4},{4,6},{6,0},{1,3},{3,5},{5,7},{7,1},{8,10},{10,12},{12... | collective-permute-start | bytes 1572872 | tf_op jit(solution)/shard_map/ppermute | solution.py:38
  209.1 8.7 %collective-permute-start.14 = (bf16[64,2048]{1,0:T(8,128)(2,1)S(1)}, bf16[64,2048]{1,0:T(8,128)(2,1)S(1)}, u32[]{:S(2)}, u32[]{:S(2)}) collective-permute-start(bf16[64,2048]{1,0:T(8,128)(2,1)S(1)} %get-tuple-element.223), channel_id=1, source_target_pairs={{0,1},{1,0},{2,3},{3,2},{4,5},{5,4},{6,7},{7,6},{8,9},{9,8},{10,11... | collective-permute-start | bytes 786440 | tf_op jit(solution)/shard_map/ppermute | solution.py:38
  210.4 13.1 %collective-permute-start.22 = (bf16[64,2048]{1,0:T(8,128)(2,1)S(1)}, bf16[64,2048]{1,0:T(8,128)(2,1)S(1)}, u32[]{:S(2)}, u32[]{:S(2)}) collective-permute-start(bf16[64,2048]{1,0:T(8,128)(2,1)S(1)} %collective-permute-done.13.rest_4_), channel_id=1, source_target_pairs={{0,2},{2,4},{4,6},{6,0},{1,3},{3,5},{5,7},{7,1},{8,10},{10,12},{12... | collective-permute-start | bytes 786440 | tf_op jit(solution)/shard_map/ppermute | solution.py:38
  211.2 12.2 %collective-permute-start.17 = (bf16[64,2048]{1,0:T(8,128)(2,1)S(1)}, bf16[64,2048]{1,0:T(8,128)(2,1)S(1)}, u32[]{:S(2)}, u32[]{:S(2)}) collective-permute-start(bf16[64,2048]{1,0:T(8,128)(2,1)S(1)} %slice.181), channel_id=1, source_target_pairs={{0,1},{1,0},{2,3},{3,2},{4,5},{5,4},{6,7},{7,6},{8,9},{9,8},{10,11... | collective-permute-start | bytes 786440 | tf_op jit(solution)/shard_map/ppermute | solution.py:38
  212.4 11.9 %collective-permute-start.23 = (bf16[64,2048]{1,0:T(8,128)(2,1)S(1)}, bf16[64,2048]{1,0:T(8,128)(2,1)S(1)}, u32[]{:S(2)}, u32[]{:S(2)}) collective-permute-start(bf16[64,2048]{1,0:T(8,128)(2,1)S(1)} %slice.183), channel_id=1, source_target_pairs={{0,1},{1,0},{2,3},{3,2},{4,5},{5,4},{6,7},{7,6},{8,9},{9,8},{10,11... | collective-permute-start | bytes 786440 | tf_op jit(solution)/shard_map/ppermute | solution.py:38
  217.8 12.1 %collective-permute-start.21 = (bf16[64,2048]{1,0:T(8,128)(2,1)S(1)}, bf16[64,2048]{1,0:T(8,128)(2,1)S(1)}, u32[]{:S(2)}, u32[]{:S(2)}) collective-permute-start(bf16[64,2048]{1,0:T(8,128)(2,1)S(1)} %slice.182), channel_id=1, source_target_pairs={{0,1},{1,0},{2,3},{3,2},{4,5},{5,4},{6,7},{7,6},{8,9},{9,8},{10,11... | collective-permute-start | bytes 786440 | tf_op jit(solution)/shard_map/ppermute | solution.py:38
  256.8 51.8 %all-to-all-start.2 = ((bf16[8,128,2048]{2,1,0:T(8,128)(2,1)}), bf16[8,128,2048]{2,1,0:T(8,128)(2,1)}, u32[]{:S(2)}, u32[]{:S(2)}) async-start(bf16[8,128,2048]{2,1,0:T(8,128)(2,1)} %bitcast.96), calls=%async_computation.2 | async-start | bytes 8388608 | tf_op jit(solution)/shard_map/all_to_all | solution.py:103
  262.5 130.7 %reduce-scatter.2.cloned.1.call-start = ((), (), s32[]{:S(2)}) async-start(), calls=%async_computation.6 | async-start | bytes 10616832 | tf_op jit(solution)/shard_map/reduce_scatter | solution.py:94
  312.4 10.4 %collective-permute-start.29 = (bf16[128,2048]{1,0:T(8,128)(2,1)S(1)}, bf16[128,2048]{1,0:T(8,128)(2,1)S(1)}, u32[]{:S(2)}, u32[]{:S(2)}) collective-permute-start(bf16[128,2048]{1,0:T(8,128)(2,1)S(1)} %get-tuple-element.211.rest_0_), channel_id=1, source_target_pairs={{0,2},{2,4},{4,6},{6,0},{1,3},{3,5},{5,7},{7,1},{8,10},{10,12},{12... | collective-permute-start | bytes 1572872 | tf_op jit(solution)/shard_map/ppermute | solution.py:38
  312.6 27.7 %collective-permute-start.26 = (bf16[128,2048]{1,0:T(8,128)(2,1)S(1)}, bf16[128,2048]{1,0:T(8,128)(2,1)S(1)}, u32[]{:S(2)}, u32[]{:S(2)}) collective-permute-start(bf16[128,2048]{1,0:T(8,128)(2,1)S(1)} %get-tuple-element.211.rest_0_), channel_id=1, source_target_pairs={{0,6},{2,0},{4,2},{6,4},{1,7},{3,1},{5,3},{7,5},{8,14},{10,8},{12,... | collective-permute-start | bytes 1572872 | tf_op jit(solution)/shard_map/ppermute | solution.py:38
  322.8 22.5 %collective-permute-start.30 = (bf16[128,2048]{1,0:T(8,128)(2,1)S(1)}, bf16[128,2048]{1,0:T(8,128)(2,1)S(1)}, u32[]{:S(2)}, u32[]{:S(2)}) collective-permute-start(bf16[128,2048]{1,0:T(8,128)(2,1)S(1)} %collective-permute-done.29.rest_9_), channel_id=1, source_target_pairs={{0,2},{2,4},{4,6},{6,0},{1,3},{3,5},{5,7},{7,1},{8,10},{10,12},{12... | collective-permute-start | bytes 1572872 | tf_op jit(solution)/shard_map/ppermute | solution.py:38
  322.8 19.1 %collective-permute-start.27 = (bf16[64,2048]{1,0:T(8,128)(2,1)S(1)}, bf16[64,2048]{1,0:T(8,128)(2,1)}, u32[]{:S(2)}, u32[]{:S(2)}) collective-permute-start(bf16[64,2048]{1,0:T(8,128)(2,1)S(1)} %collective-permute-done.24.rest_1_), channel_id=1, source_target_pairs={{0,6},{2,0},{4,2},{6,4},{1,7},{3,1},{5,3},{7,5},{8,14},{10,8},{12,... | collective-permute-start | bytes 786440 | tf_op jit(solution)/shard_map/ppermute | solution.py:38
  334.1 13.4 %collective-permute-start.25 = (bf16[64,2048]{1,0:T(8,128)(2,1)S(1)}, bf16[64,2048]{1,0:T(8,128)(2,1)}, u32[]{:S(2)}, u32[]{:S(2)}) collective-permute-start(bf16[64,2048]{1,0:T(8,128)(2,1)S(1)} %get-tuple-element.221), channel_id=1, source_target_pairs={{0,1},{1,0},{2,3},{3,2},{4,5},{5,4},{6,7},{7,6},{8,9},{9,8},{10,11... | collective-permute-start | bytes 786440 | tf_op jit(solution)/shard_map/ppermute | solution.py:38
  339.8 8.3 %collective-permute-start.33 = (bf16[64,2048]{1,0:T(8,128)(2,1)S(1)}, bf16[64,2048]{1,0:T(8,128)(2,1)}, u32[]{:S(2)}, u32[]{:S(2)}) collective-permute-start(bf16[64,2048]{1,0:T(8,128)(2,1)S(1)} %collective-permute-done.24.rest_1_), channel_id=1, source_target_pairs={{0,2},{2,4},{4,6},{6,0},{1,3},{3,5},{5,7},{7,1},{8,10},{10,12},{12... | collective-permute-start | bytes 786440 | tf_op jit(solution)/shard_map/ppermute | solution.py:38
  341.1 10.1 %collective-permute-start.28 = (bf16[64,2048]{1,0:T(8,128)(2,1)}, bf16[64,2048]{1,0:T(8,128)(2,1)}, u32[]{:S(2)}, u32[]{:S(2)}) collective-permute-start(bf16[64,2048]{1,0:T(8,128)(2,1)} %slice.186), channel_id=1, source_target_pairs={{0,1},{1,0},{2,3},{3,2},{4,5},{5,4},{6,7},{7,6},{8,9},{9,8},{10,11... | collective-permute-start | bytes 786440 | tf_op jit(solution)/shard_map/ppermute | solution.py:38
  341.8 13.5 %collective-permute-start.34 = (bf16[64,2048]{1,0:T(8,128)(2,1)}, bf16[64,2048]{1,0:T(8,128)(2,1)}, u32[]{:S(2)}, u32[]{:S(2)}) collective-permute-start(bf16[64,2048]{1,0:T(8,128)(2,1)} %slice.188), channel_id=1, source_target_pairs={{0,1},{1,0},{2,3},{3,2},{4,5},{5,4},{6,7},{7,6},{8,9},{9,8},{10,11... | collective-permute-start | bytes 786440 | tf_op jit(solution)/shard_map/ppermute | solution.py:38
  347.4 13.5 %collective-permute-start.32 = (bf16[64,2048]{1,0:T(8,128)(2,1)}, bf16[64,2048]{1,0:T(8,128)(2,1)}, u32[]{:S(2)}, u32[]{:S(2)}) collective-permute-start(bf16[64,2048]{1,0:T(8,128)(2,1)} %slice.187), channel_id=1, source_target_pairs={{0,1},{1,0},{2,3},{3,2},{4,5},{5,4},{6,7},{7,6},{8,9},{9,8},{10,11... | collective-permute-start | bytes 786440 | tf_op jit(solution)/shard_map/ppermute | solution.py:38
  361.0 50.9 %all-to-all-start.3 = ((bf16[8,128,2048]{2,1,0:T(8,128)(2,1)}), bf16[8,128,2048]{2,1,0:T(8,128)(2,1)}, u32[]{:S(2)}, u32[]{:S(2)}) async-start(bf16[8,128,2048]{2,1,0:T(8,128)(2,1)} %bitcast.93), calls=%async_computation.3 | async-start | bytes 8388608 | tf_op jit(solution)/shard_map/all_to_all | solution.py:103
  408.4 18.0 %collective-permute-start.35 = (bf16[8,128,1664]{2,1,0:T(8,128)(2,1)}, bf16[8,128,1664]{2,1,0:T(8,128)(2,1)}, u32[]{:S(2)}, u32[]{:S(2)}) collective-permute-start(bf16[8,128,1664]{2,1,0:T(8,128)(2,1)} %get-tuple-element.180), channel_id=1, source_target_pairs={{0,8},{8,0},{1,9},{9,1},{2,10},{10,2},{3,11},{11,3},{4,12},{12,4},... | collective-permute-start | bytes 10223624 | tf_op jit(solution)/shard_map/ppermute | solution.py:38
  411.9 53.1 %all-to-all-start.4 = ((bf16[8,128,2048]{2,1,0:T(8,128)(2,1)}), bf16[8,128,2048]{2,1,0:T(8,128)(2,1)}, u32[]{:S(2)}, u32[]{:S(2)}) async-start(bf16[8,128,2048]{2,1,0:T(8,128)(2,1)} %bitcast.94), calls=%async_computation.4 | async-start | bytes 8388608 | tf_op jit(solution)/shard_map/all_to_all | solution.py:103
  429.4 11.5 %collective-permute-start.37 = (bf16[128,1664]{1,0:T(8,128)(2,1)S(1)}, bf16[128,1664]{1,0:T(8,128)(2,1)S(1)}, u32[]{:S(2)}, u32[]{:S(2)}) collective-permute-start(bf16[128,1664]{1,0:T(8,128)(2,1)S(1)} %get-tuple-element.219), channel_id=1, source_target_pairs={{0,48},{16,0},{32,16},{48,32},{1,49},{17,1},{33,17},{49,33},{2,50}... | collective-permute-start | bytes 1277960 | tf_op jit(solution)/shard_map/ppermute | solution.py:38
  429.4 12.8 %collective-permute-start.46 = (bf16[128,1664]{1,0:T(8,128)(2,1)S(1)}, bf16[128,1664]{1,0:T(8,128)(2,1)S(1)}, u32[]{:S(2)}, u32[]{:S(2)}) collective-permute-start(bf16[128,1664]{1,0:T(8,128)(2,1)S(1)} %get-tuple-element.217), channel_id=1, source_target_pairs={{0,16},{16,32},{32,48},{48,0},{1,17},{17,33},{33,49},{49,1},{2,18}... | collective-permute-start | bytes 1277960 | tf_op jit(solution)/shard_map/ppermute | solution.py:38
  431.9 12.9 %collective-permute-start.40 = (f32[64,128]{1,0:T(8,128)S(1)}, f32[64,128]{1,0:T(8,128)S(1)}, u32[]{:S(2)}, u32[]{:S(2)}) collective-permute-start(f32[64,128]{1,0:T(8,128)S(1)} %fusion.36), channel_id=1, source_target_pairs={{0,16},{16,0},{32,48},{48,32},{1,17},{17,1},{33,49},{49,33},{2,18}... | collective-permute-start | bytes 98312 | tf_op jit(solution)/shard_map/ppermute | solution.py:133
  432.0 25.6 %collective-permute-start.36 = (bf16[128,1664]{1,0:T(8,128)(2,1)S(1)}, bf16[128,1664]{1,0:T(8,128)(2,1)S(1)}, u32[]{:S(2)}, u32[]{:S(2)}) collective-permute-start(bf16[128,1664]{1,0:T(8,128)(2,1)S(1)} %get-tuple-element.220), channel_id=1, source_target_pairs={{0,16},{16,32},{32,48},{48,0},{1,17},{17,33},{33,49},{49,1},{2,18}... | collective-permute-start | bytes 1277960 | tf_op jit(solution)/shard_map/ppermute | solution.py:38
  444.7 12.9 %collective-permute-start.38 = (bf16[128,1664]{1,0:T(8,128)(2,1)S(1)}, bf16[128,1664]{1,0:T(8,128)(2,1)S(1)}, u32[]{:S(2)}, u32[]{:S(2)}) collective-permute-start(bf16[128,1664]{1,0:T(8,128)(2,1)S(1)} %get-tuple-element.216), channel_id=1, source_target_pairs={{0,48},{16,0},{32,16},{48,32},{1,49},{17,1},{33,17},{49,33},{2,50}... | collective-permute-start | bytes 1277960 | tf_op jit(solution)/shard_map/ppermute | solution.py:38
  451.3 55.5 %collective-permute-start.48 = (bf16[128,1664]{1,0:T(8,128)(2,1)}, bf16[128,1664]{1,0:T(8,128)(2,1)}, u32[]{:S(2)}, u32[]{:S(2)}) collective-permute-start(bf16[128,1664]{1,0:T(8,128)(2,1)} %get-tuple-element.218), channel_id=1, source_target_pairs={{0,48},{16,0},{32,16},{48,32},{1,49},{17,1},{33,17},{49,33},{2,50}... | collective-permute-start | bytes 1277960 | tf_op jit(solution)/shard_map/ppermute | solution.py:38
  457.5 49.2 %collective-permute-start.47 = (bf16[128,1664]{1,0:T(8,128)(2,1)}, bf16[128,1664]{1,0:T(8,128)(2,1)}, u32[]{:S(2)}, u32[]{:S(2)}) collective-permute-start(bf16[128,1664]{1,0:T(8,128)(2,1)} %get-tuple-element.215), channel_id=1, source_target_pairs={{0,16},{16,32},{32,48},{48,0},{1,17},{17,33},{33,49},{49,1},{2,18}... | collective-permute-start | bytes 1277960 | tf_op jit(solution)/shard_map/ppermute | solution.py:38
  465.0 48.3 %collective-permute-start.50 = (bf16[128,2304]{1,0:T(8,128)(2,1)}, bf16[128,2304]{1,0:T(8,128)(2,1)S(1)}, u32[]{:S(2)}, u32[]{:S(2)}) collective-permute-start(bf16[128,2304]{1,0:T(8,128)(2,1)} %dynamic-slice_bitcast_fusion), channel_id=1, source_target_pairs={{0,64},{64,0},{1,65},{65,1},{2,66},{66,2},{3,67},{67,3},{4,68},{68... | collective-permute-start | bytes 1769480 | tf_op jit(solution)/shard_map/ppermute | solution.py:38
  467.6 39.2 %collective-permute-start.49 = (bf16[128,1664]{1,0:T(8,128)(2,1)}, bf16[128,1664]{1,0:T(8,128)(2,1)}, u32[]{:S(2)}, u32[]{:S(2)}) collective-permute-start(bf16[128,1664]{1,0:T(8,128)(2,1)} %fusion.12), channel_id=1, source_target_pairs={{0,64},{64,0},{1,65},{65,1},{2,66},{66,2},{3,67},{67,3},{4,68},{68... | collective-permute-start | bytes 1277960 | tf_op jit(solution)/shard_map/ppermute | solution.py:38
  468.2 20.0 %collective-permute-start.42 = (f32[64,128]{1,0:T(8,128)S(1)}, f32[64,128]{1,0:T(8,128)S(1)}, u32[]{:S(2)}, u32[]{:S(2)}) collective-permute-start(f32[64,128]{1,0:T(8,128)S(1)} %add.259), channel_id=1, source_target_pairs={{0,64},{64,0},{1,65},{65,1},{2,66},{66,2},{3,67},{67,3},{4,68},{68... | collective-permute-start | bytes 98312 | tf_op jit(solution)/shard_map/ppermute | solution.py:133
  (58 other events, 1357.2 us)
Sparse Core Ops, SparseCore 0:
  38.3 43.7 all-gather.4
  83.7 54.2 all-gather.6
  308.7 57.9 reduce-scatter.1
